TPU v7x, 32 devices: a whole 2x2x4 slice. The times are simulated.
32 devices in a mesh: groups: 2 (over x), blk: 16 (over z, y, core).
Axes of the slice: x: 2, y: 2, z: 4, core: 2. Of those that a mesh axis runs over, the one named last changes fastest.
Arguments:
- projections: bfloat16 [2, 512, 8192], P(None, ('groups', 'blk')), parts along dimension 1, may hold values from -12 to 12
- images: bfloat16 [64, 8192], P(('groups', 'blk')), parts along dimension 0, may hold values from -16 to 16, as said below
- ctf_group: int32 [64], P(('groups', 'blk')), parts along dimension 0, may hold values from 0 to 15
- shift_offsets: int32 [64, 9, 2], P(('groups', 'blk')), parts along dimension 0, may hold values from -8 to 8
- shell_limit: int32 [64], P(('groups', 'blk')), parts along dimension 0, may hold values from 16 to 63
- ctf_table: float32 [32, 4096], P('groups'), parts along dimension 0, may hold values from -1 to 1
- noise_weight: float32 [32, 4096], P('groups'), parts along dimension 0, may hold values from 0.25 to 4
Outputs:
- slices: float32 [2, 512, 8192], P(None, ('groups', 'blk')), parts along dimension 1
- best_posterior: float32 [64], P(('groups', 'blk')), parts along dimension 0
- log_total: float32 [64], P(('groups', 'blk')), parts along dimension 0
There are 2 independent parts, one for each index of `groups`. A program takes and returns all parts, laid end to end along the dimension named above; each array names one. Nothing has to cross between parts.
Inputs may be any that keep to these rules, and one draw needn't show every extreme that they name: `images`: image coefficients.
All inputs are finite; a program needn't handle non-finite values.
Results may differ from a plain program's by a relative error of at most 0.006.
Values may be sent and summed in bfloat16 or wider, within the bound.
A program may use at most 128 MiB of HBM per device.

v0:
```python
import math

import jax
import jax.numpy as jnp
from jax import lax
from jax.sharding import PartitionSpec as P

KY = 64
IMG = 256


def combined_all(value, axis, join):
    pieces = jax.tree.map(lambda part: lax.all_gather(part, axis), value)
    head = jax.tree.map(lambda part: part[0], pieces)
    tail = jax.tree.map(lambda part: part[1:], pieces)
    so_far, _ = lax.scan(lambda so_far, section: (join(so_far, section), None), head, tail)
    return so_far


def frequencies(half_width):
    positions = jnp.arange(half_width, dtype=jnp.int32)
    return (positions // KY, positions % KY - KY // 2)


def shift_factors(offsets, half_width):
    row_count = offsets.shape[0]
    shift_count = offsets.shape[1]
    row_freq = jnp.arange(half_width // KY, dtype=jnp.int32)
    col_freq = jnp.arange(KY, dtype=jnp.int32) - KY // 2
    turns_x = row_freq[None, None, :] * offsets[:, :, 0:1] % IMG
    turns_y = col_freq[None, None, :] * offsets[:, :, 1:2] % IMG
    angle_x = turns_x.astype(jnp.float32) * (2.0 * math.pi / IMG)
    angle_y = turns_y.astype(jnp.float32) * (2.0 * math.pi / IMG)
    cosine_x = jnp.cos(angle_x)[:, :, :, None]
    sine_x = jnp.sin(angle_x)[:, :, :, None]
    cosine_y = jnp.cos(angle_y)[:, :, None, :]
    sine_y = jnp.sin(angle_y)[:, :, None, :]
    cosine = cosine_x * cosine_y - sine_x * sine_y
    sine_part = sine_x * cosine_y + cosine_x * sine_y
    return (
        cosine.reshape(row_count, shift_count, half_width),
        sine_part.reshape(row_count, shift_count, half_width),
    )


def particle_terms(image_rows, ctf_rows, weight_rows, offsets, limits, freq_x, freq_y):
    half_width = image_rows.shape[1] // 2
    image_real = image_rows[:, :half_width].astype(jnp.float32)
    image_imag = image_rows[:, half_width:].astype(jnp.float32)
    radius_sq = freq_x * freq_x + freq_y * freq_y
    inside = (radius_sq[None, :] < (limits * limits)[:, None]).astype(jnp.float32)
    masked_weight = inside * weight_rows
    ctf_weight = masked_weight * ctf_rows
    norm_term = jnp.sum(masked_weight * (image_real * image_real + image_imag * image_imag), axis=1)
    quad_weight = ctf_weight * ctf_rows
    cosine, sine_part = shift_factors(offsets, half_width)
    shift_real = image_real[:, None, :] * cosine + image_imag[:, None, :] * sine_part
    shift_imag = image_imag[:, None, :] * cosine - image_real[:, None, :] * sine_part
    weighted = jnp.concatenate(
        [ctf_weight[:, None, :] * shift_real, ctf_weight[:, None, :] * shift_imag], axis=2
    ).astype(jnp.bfloat16)
    return (weighted, norm_term, quad_weight)


def combine_lse(first, second):
    score_top = jnp.maximum(first[0], second[0])
    exp_total = first[1] * jnp.exp(first[0] - score_top) + second[1] * jnp.exp(
        second[0] - score_top
    )
    return (score_top, exp_total)


def block_shape(row_count):
    return 64 if row_count % 64 == 0 else row_count


def split_rows(members, block_rows):
    return tuple(
        (
            member.reshape((member.shape[0] // block_rows, block_rows) + member.shape[1:])
            for member in members
        )
    )


def local(projections, images, ctf_group, shift_offsets, shell_limit, ctf_table, noise_weight):
    batch_count, orient_dev, full_width = projections.shape
    half_width = full_width // 2
    candidates = batch_count * orient_dev
    flat_proj = projections.reshape(candidates, full_width)
    proj_real = flat_proj[:, :half_width].astype(jnp.float32)
    proj_imag = flat_proj[:, half_width:].astype(jnp.float32)
    proj_power = proj_real * proj_real + proj_imag * proj_imag
    freq_x, freq_y = frequencies(half_width)
    score_scale = 0.5 / math.sqrt(half_width)
    group_count = ctf_table.shape[0]
    particles_dev = images.shape[0]

    def block_terms(members):
        image_rows, groups, offsets, limits = members
        one_hot = (groups[:, None] == jnp.arange(group_count, dtype=jnp.int32)[None, :]).astype(
            jnp.float32
        )
        ctf_rows = jnp.dot(
            one_hot, ctf_table, precision=lax.Precision.HIGHEST, preferred_element_type=jnp.float32
        )
        weight_rows = jnp.dot(
            one_hot,
            noise_weight,
            precision=lax.Precision.HIGHEST,
            preferred_element_type=jnp.float32,
        )
        return particle_terms(image_rows, ctf_rows, weight_rows, offsets, limits, freq_x, freq_y)

    def score_block(members):
        weighted, norm_term, quad_weight = block_terms(members)
        cross_term = lax.dot_general(
            weighted, flat_proj, (((2,), (1,)), ((), ())), preferred_element_type=jnp.float32
        )
        quad_term = lax.dot_general(
            quad_weight,
            proj_power,
            (((1,), (1,)), ((), ())),
            precision=lax.Precision.HIGHEST,
            preferred_element_type=jnp.float32,
        )
        return -(norm_term[:, None, None] - 2.0 * cross_term + quad_term[:, None, :]) * score_scale

    members = (
        lax.all_gather(images, "blk", axis=0, tiled=True),
        lax.all_gather(ctf_group, "blk", axis=0, tiled=True),
        lax.all_gather(shift_offsets, "blk", axis=0, tiled=True),
        lax.all_gather(shell_limit, "blk", axis=0, tiled=True),
    )
    row_count = members[0].shape[0]
    block_rows = block_shape(row_count)
    blocks = lax.map(score_block, split_rows(members, block_rows))
    scores = blocks.reshape((row_count,) + blocks.shape[2:])
    local_top = jnp.max(scores, axis=(1, 2))
    local_total = jnp.sum(jnp.exp(scores - local_top[:, None, None]), axis=(1, 2))
    score_top, exp_total = combined_all((local_top, local_total), "blk", combine_lse)
    log_total = score_top + jnp.log(exp_total)
    pieces = (
        lax.all_gather(images, "blk", axis=0, tiled=True),
        lax.all_gather(ctf_group, "blk", axis=0, tiled=True),
        lax.all_gather(shift_offsets, "blk", axis=0, tiled=True),
        lax.all_gather(shell_limit, "blk", axis=0, tiled=True),
    )
    row_count = pieces[0].shape[0]
    block_rows = block_shape(row_count)

    def add_block(carry, packed):
        member_block, score_block_values, log_block = packed
        weighted = block_terms(member_block)[0]
        posterior = jnp.exp(score_block_values - log_block[:, None, None]).astype(jnp.bfloat16)
        contrib = lax.dot_general(
            posterior, weighted, (((0, 1), (0, 1)), ((), ())), preferred_element_type=jnp.float32
        )
        return (carry + contrib, None)

    zero_slices = jnp.zeros((candidates, full_width), jnp.float32)
    packed_scores = split_rows((scores, log_total), block_rows)
    summed, unused_out = lax.scan(
        add_block, zero_slices, (split_rows(pieces, block_rows), packed_scores[0], packed_scores[1])
    )
    slices = (summed * (candidates / particles_dev)).reshape(batch_count, orient_dev, full_width)
    own_start = lax.axis_index("blk") * particles_dev
    own_top = lax.dynamic_slice_in_dim(score_top, own_start, particles_dev, 0)
    own_log = lax.dynamic_slice_in_dim(log_total, own_start, particles_dev, 0)
    best_posterior = jnp.exp(own_top - own_log)
    return (slices, best_posterior, own_log)


def solution(mesh):
    in_specs = (
        P(None, ("groups", "blk"), None),
        P(("groups", "blk"), None),
        P(("groups", "blk")),
        P(("groups", "blk"), None, None),
        P(("groups", "blk")),
        P("groups", None),
        P("groups", None),
    )
    out_specs = (P(None, ("groups", "blk"), None), P(("groups", "blk")), P(("groups", "blk")))
    return jax.shard_map(local, mesh=mesh, in_specs=in_specs, out_specs=out_specs, check_vma=False)
```

profile of v0, /device:TPU:0, one launch (start us, length us, event | category | flops | bytes accessed | tf_op | source)
XLA Modules:
  0.0 127.0 jit_solution(18370479021721928491)
XLA Ops:
  0.6 0.0 copy-start
  0.6 23.6 %all_gather.31 = s32[32,9,2]{1,2,0:T(2,128)S(1)} all-gather(s32[2,9,2]{1,2,0:T(2,128)} %param.12), channel_id=1, replica_groups=mesh['groups'=2,'blk'=16] {'blk'}, dimensions={0}, use_global_device_ids=true | all-gather | bytes 2448 | tf_op jit(solution)/shard_map/all_gather | solution.py:146
  24.2 0.1 copy.14
  24.3 0.1 copy.13
  24.4 1.2 fusion.32
  25.6 7.2 %multiply_subtract_fusion = (f32[32,9,64,64]{3,2,0,1:T(8,128)}, f32[32,9,64,64]{3,2,0,1:T(8,128)}) fusion(f32[32,9,64]{2,0,1:T(8,128)S(1)} %get-tuple-element.134, f32[32,9,64]{2,0,1:T(8,128)S(1)} %get-tuple-element.140, f32[32,9,64]{2,0,1:T(8,128)S(1)} %get-tuple-element.133, f32[32,9,64]{2,0,1:T(8,128)S(1)} %get-tuple-element.141), kind=kLoop, calls=%fused_computation.8 | loop fusion | flops 7077888 | bytes 9732096 | tf_op jit(solution)/shard_map/while/body/eval_jaxpr/sub | solution.py:38
  32.8 8.3 %add.127 = f32[32,9,4096]{2,0,1:T(8,128)} reshape(f32[32,9,64,64]{3,2,0,1:T(8,128)} %get-tuple-element.126) | data formatting | bytes 9437184 | tf_op jit(solution)/shard_map/while/body/eval_jaxpr/add | solution.py:39
  41.1 0.0 copy-start.4
  41.1 0.0 copy-start.7
  41.1 0.0 copy-start.5
  41.1 0.0 copy-start.6
  41.1 0.0 copy-start.2
  41.1 8.4 %sub.78 = f32[32,9,4096]{2,0,1:T(8,128)} reshape(f32[32,9,64,64]{3,2,0,1:T(8,128)} %get-tuple-element.125) | data formatting | bytes 9437184 | tf_op jit(solution)/shard_map/while/body/eval_jaxpr/sub | solution.py:38
  49.5 0.0 copy-done.4
  49.5 18.8 %all-gather.2 = bf16[16,2,8192]{2,1,0:T(2,128)(2,1)S(1)} all-gather(bf16[1,2,8192]{2,1,0:T(2,128)(2,1)S(1)} %bitcast.43), channel_id=1, replica_groups=mesh['groups'=2,'blk'=16] {'blk'}, dimensions={0}, use_global_device_ids=true | all-gather | bytes 557056 | tf_op jit(solution)/shard_map/all_gather | solution.py:144
  68.3 0.2 reshape.156
  68.5 0.9 slice_convert_fusion.1
  69.4 0.0 copy-done.7
  69.4 0.6 dynamic-slice.6
  70.7 0.0 copy-done.5
  70.7 0.2 dynamic-update-slice
  70.9 0.0 copy-done.6
  70.9 0.2 dynamic-update-slice.1
  71.1 9.5 %all-reduce.4 = (s32[32]{0:T(128)S(1)}, s32[32]{0:T(128)S(1)}) all-reduce(s32[32]{0:T(128)S(1)} %dynamic-update-slice, s32[32]{0:T(128)S(1)} %dynamic-update-slice.1), channel_id=1, replica_groups=mesh['groups'=2,'blk'=16] {'blk'}, use_global_device_ids=true, to_apply=%add | all-reduce | flops 64 | bytes 512
  80.6 0.0 copy-done.2
  80.6 0.4 fusion.46
  81.0 0.0 copy-done
  81.1 0.6 multiply_reduce_fusion
  81.7 0.0 copy-start.3
  81.7 4.7 %multiply_convert_fusion.1 = (bf16[32,9,4096]{2,0,1:T(8,128)(2,1)S(1)}, bf16[32,9,4096]{2,0,1:T(8,128)(2,1)S(1)}) fusion(f32[32,9,4096]{2,0,1:T(8,128)} %add.127, f32[32,9,4096]{2,0,1:T(8,128)} %sub.78, f32[32,4096]{1,0:T(8,128)} %get-tuple-element.130, f32[32,4096]{1,0:T(8,128)S(1)} %get-tuple-element.129, f32[32,4096]{1,0:T(8,128)S(1)} %get-tuple-element.128), kind=kLoop, calls=%fused_computation.13 | loop fusion | flops 11796480 | bytes 15728640 | tf_op jit(solution)/shard_map/convert
  86.3 0.0 copy-start.1
  86.4 0.0 copy-done.3
  86.4 0.6 fusion.12
  87.0 3.5 %fusion.53 = (f32[32]{0:T(128)S(1)}, f32[32,9,32]{0,2,1:T(8,128)S(1)}) fusion(f32[32,32]{0,1:T(8,128)S(1)} %fusion.12, bf16[32,8192,1]{1,0,2:T(8,128)(2,1)S(1)} %bitcast.40, bf16[32,9,4096]{2,0,1:T(8,128)(2,1)S(1)} %get-tuple-element.124, bf16[32,9,4096]{2,0,1:T(8,128)(2,1)S(1)} %get-tuple-element.123, f32[32]{0:T(128)S(1)} %get-tuple-element.127), kind=kOutput, calls=%fused_computation.82 | convolution fusion | flops 160487392 | bytes 5284096 | tf_op jit(solution)/shard_map/while/body/eval_jaxpr/dot_general | solution.py:117
  90.5 0.0 copy-done.1
  91.2 0.2 dynamic-update-slice.2
  91.4 0.1 exponential_reduce_fusion
  91.5 0.2 dynamic-update-slice.3
  91.7 30.1 %all-reduce.5 = (f32[512]{0:T(512)S(1)}, f32[512]{0:T(512)S(1)}) all-reduce(f32[512]{0:T(512)S(1)} %dynamic-update-slice.2, f32[512]{0:T(512)S(1)} %dynamic-update-slice.3), channel_id=2, replica_groups=mesh['groups'=2,'blk'=16] {'blk'}, use_global_device_ids=true, to_apply=%add.2 | all-reduce | flops 1024 | bytes 8192
  121.8 0.1 slice.54
  121.9 0.1 reshape.141
  122.0 0.1 slice.55
  122.0 0.1 reshape.142
  122.1 0.6 while.2
  122.7 3.6 %fusion.5 = f32[32,8192]{1,0:T(8,128)} fusion(bf16[32,9,4096]{2,0,1:T(8,128)(2,1)} %copy-done.1, bf16[32,9,4096]{2,0,1:T(8,128)(2,1)S(1)} %get-tuple-element.123, f32[32,9,32]{0,2,1:T(8,128)S(1)} %get-tuple-element.139, f32[32]{0:T(128)S(1)} %log_add_fusion), kind=kOutput, calls=%fused_computation.10 | convolution fusion | flops 160712704 | bytes 5804160 | tf_op jit(solution)/shard_map/while/body/eval_jaxpr/dot_general | solution.py:156
  126.4 0.6 subtract_exponential_fusion
  (26 shorter events, 0.5 us)
Async XLA Ops:
  0.6 80.4 %copy-start = (f32[16,4096]{1,0:T(8,128)S(1)}, f32[16,4096]{1,0:T(8,128)}, u32[]{:S(2)}) copy-start(f32[16,4096]{1,0:T(8,128)} %param.15) | copy-start | bytes 786436
  41.1 8.4 %copy-start.4 = (bf16[2,8192]{1,0:T(2,128)(2,1)S(1)}, bf16[2,8192]{1,0:T(2,128)(2,1)}, u32[]{:S(2)}) copy-start(bf16[2,8192]{1,0:T(2,128)(2,1)} %param.10) | copy-start | bytes 98308
  41.1 28.3 %copy-start.7 = (u32[32]{0:T(128)S(1)}, u32[32]{0:T(128)}, u32[]{:S(2)}) copy-start(u32[32]{0:T(128)} %constant.138) | copy-start | bytes 388
  41.1 29.5 %copy-start.5 = (s32[2]{0:T(128)S(1)}, s32[2]{0:T(128)}, u32[]{:S(2)}) copy-start(s32[2]{0:T(128)} %param.13) | copy-start | bytes 28
  41.1 29.8 %copy-start.6 = (s32[2]{0:T(128)S(1)}, s32[2]{0:T(128)}, u32[]{:S(2)}) copy-start(s32[2]{0:T(128)} %param.11) | copy-start | bytes 28
  41.1 39.5 %copy-start.2 = (f32[16,4096]{1,0:T(8,128)S(1)}, f32[16,4096]{1,0:T(8,128)}, u32[]{:S(2)}) copy-start(f32[16,4096]{1,0:T(8,128)} %param.14) | copy-start | bytes 786436
  81.7 4.7 %copy-start.3 = (bf16[2,16,8192]{2,1,0:T(8,128)(2,1)S(1)}, bf16[2,16,8192]{2,1,0:T(8,128)(2,1)}, u32[]{:S(2)}) copy-start(bf16[2,16,8192]{2,1,0:T(8,128)(2,1)} %param.9) | copy-start | bytes 1572868
  86.3 4.2 %copy-start.1 = (bf16[32,9,4096]{2,0,1:T(8,128)(2,1)}, bf16[32,9,4096]{2,0,1:T(8,128)(2,1)S(1)}, u32[]{:S(2)}) copy-start(bf16[32,9,4096]{2,0,1:T(8,128)(2,1)S(1)} %get-tuple-element.124) | copy-start | bytes 7077892
where the time goes:
time: 127 us
  blocking collectives  81.9 us (64%)
  local copies, waits for them, and re-layouts  18.9 us (15%)
  other arithmetic  15 us (12%)
  matrix products  8.79 us (7%)
  between operations  2.1 us (2%)
    unnamed x2, blocking collectives  39.5 us
    all_gather x1, blocking collectives, local(): lax.all_gather(shift_offsets, 'blk', axis=0, tiled=True)  23.6 us
    all_gather x1, blocking collectives, local(): lax.all_gather(images, 'blk', axis=0, tiled=True)  18.8 us
    sub x1, local copies, waits for them, and re-layouts, shift_factors(): cosine = cosine_x * cosine_y - sine_x * sine_y  8.36 us
    add x1, local copies, waits for them, and re-layouts, shift_factors(): sine_part = sine_x * cosine_y + cosine_x * sine_y  8.32 us
    sub x1, other arithmetic, shift_factors(): cosine = cosine_x * cosine_y - sine_x * sine_y  7.17 us
    another operation x1, other arithmetic  4.66 us
    dot_general x1, matrix products, add_block(): lax.dot_general(posterior, weighted, (((0, 1), (0, 1)), ((), ())), prefer...  3.63 us

commit v1 on v0

--- a/solution.py
+++ b/solution.py
@@ -1,8 +1,11 @@
+import functools
 import math
 
 import jax
 import jax.numpy as jnp
 from jax import lax
+from jax.experimental import pallas as pl
+from jax.experimental.pallas import tpu as pltpu
 from jax.sharding import PartitionSpec as P
 
 KY = 64
@@ -171,6 +174,297 @@
     return (slices, best_posterior, own_log)
 
 
+LANES = 128
+TILE_KX = LANES // KY
+VMEM_LIMIT = 48 * 1024 * 1024
+
+
+def turn_cos_sin(turns):
+    turns = turns - IMG * jnp.floor(turns * (1.0 / IMG) + 0.5)
+    half = turns * (math.pi / IMG)
+    sq = half * half
+    sin_poly = 1.0 / math.factorial(13)
+    for power in (11, 9, 7, 5, 3, 1):
+        sin_poly = sin_poly * sq + (-1.0) ** (power // 2) / math.factorial(power)
+    cos_poly = 1.0 / math.factorial(14) * -1.0
+    for power in (12, 10, 8, 6, 4, 2, 0):
+        cos_poly = cos_poly * sq + (-1.0) ** (power // 2) / math.factorial(power)
+    sin_half = sin_poly * half
+    return 1.0 - 2.0 * sin_half * sin_half, 2.0 * sin_half * cos_poly
+
+
+def three_parts(values):
+    first = values.astype(jnp.bfloat16)
+    rest = values - first.astype(jnp.float32)
+    second = rest.astype(jnp.bfloat16)
+    third = (rest - second.astype(jnp.float32)).astype(jnp.bfloat16)
+    return first, second, third
+
+
+def grid_sides(device_count):
+    chips = device_count // 2
+    outer = 2 ** ((chips.bit_length()) // 2)
+    return outer, chips // outer
+
+
+def kernel(
+    sizes,
+    proj_ref, img_ref, grp_ref, off_ref, lim_ref, ctf_ref, noise_ref,
+    out_ref, best_ref, log_ref,
+    pkt, image, power, quad_w, tabs, ec_p, es_p, ec_m, es_m, dc, ds, wbuf, cross, norm, stats,
+    send_sem, recv_sem, stat_send, stat_recv,
+):
+    n, na, nb, rows, shifts, half_width = sizes
+    own_rows = rows // n
+    full = 2 * half_width
+    tiles = half_width // LANES
+    groups = ctf_ref.shape[0]
+    me = lax.axis_index("blk")
+    core = me % 2
+    chip = me // 2
+    a, b = chip // nb, chip % nb
+
+    def at(pa, pb, pc):
+        return (pa * nb + pb) * 2 + pc
+
+    barrier = pltpu.get_barrier_semaphore()
+    for step in range(1, n):
+        pl.semaphore_signal(barrier, inc=1, device_id={"blk": (me + step) % n})
+
+    sub = lax.broadcasted_iota(jnp.int32, (own_rows, LANES), 0)
+    lane = lax.broadcasted_iota(jnp.int32, (own_rows, LANES), 1)
+    meta = jnp.zeros((own_rows, LANES), jnp.float32)
+    for p in range(own_rows):
+        entries = [off_ref[p, s, j] for s in range(shifts) for j in range(2)]
+        entries += [grp_ref[p], lim_ref[p]]
+        for column, entry in enumerate(entries):
+            meta = jnp.where((sub == p) & (lane == column), entry.astype(jnp.float32), meta)
+    pkt[me, :, :full] = img_ref[...]
+    pkt[me, :, full:] = meta.astype(jnp.bfloat16)
+
+    pl.semaphore_wait(barrier, n - 1)
+
+    sends = []
+
+    def send(slot, target):
+        copy = pltpu.make_async_remote_copy(
+            src_ref=pkt.at[slot], dst_ref=pkt.at[slot],
+            send_sem=send_sem.at[len(sends)], recv_sem=recv_sem.at[slot],
+            device_id={"blk": target},
+        )
+        copy.start()
+        sends.append(copy)
+
+    def arrived(slot):
+        pltpu.make_async_remote_copy(
+            src_ref=pkt.at[slot], dst_ref=pkt.at[slot],
+            send_sem=send_sem.at[0], recv_sem=recv_sem.at[slot],
+            device_id={"blk": (me + 1) % n},
+        ).wait_recv()
+
+    other = me + 1 - 2 * core
+    for j in range(1, na):
+        send(me, at((a + j) % na, b, core))
+    for k in range(1, nb):
+        send(me, at(a, (b + k) % nb, core))
+    send(me, other)
+
+    for which, ref in enumerate((ctf_ref, noise_ref)):
+        for part, value in enumerate(three_parts(ref[...])):
+            tabs[part * groups:(part + 1) * groups, which * half_width:(which + 1) * half_width] = value
+    proj_rows = proj_ref.shape[1]
+    for batch in range(proj_ref.shape[0]):
+        real = proj_ref[batch, :, :half_width].astype(jnp.float32)
+        imag = proj_ref[batch, :, half_width:].astype(jnp.float32)
+        power[batch * proj_rows:(batch + 1) * proj_rows, :] = real * real + imag * imag
+
+    for j in range(1, na):
+        slot = at((a + na - j) % na, b, core)
+        arrived(slot)
+        for k in range(1, nb):
+            send(slot, at(a, (b + k) % nb, core))
+        send(slot, other)
+    for k in range(1, nb):
+        for j in range(na):
+            slot = at((a + na - j) % na, (b + nb - k) % nb, core)
+            arrived(slot)
+            send(slot, other)
+    for k in range(nb):
+        for j in range(na):
+            arrived(at((a + na - j) % na, (b + nb - k) % nb, 1 - core))
+
+    for d in range(n):
+        image[d * own_rows:(d + 1) * own_rows, :] = pkt[d].astype(jnp.float32)
+
+    lane = lax.broadcasted_iota(jnp.int32, (rows, LANES), 1)
+    sub = lax.broadcasted_iota(jnp.int32, (rows, LANES), 0)
+    side = lane // KY
+    freq_y = lane % KY - KY // 2
+    side_f, freq_yf = side.astype(jnp.float32), freq_y.astype(jnp.float32)
+    meta = image[:, full:]
+
+    def column(j):
+        return jnp.broadcast_to(meta[:, j:j + 1], (rows, LANES))
+
+    middle = TILE_KX * (tiles // 2)
+    for s in range(shifts):
+        at_rows = slice(s * rows, (s + 1) * rows)
+        off_x, off_y = column(2 * s), column(2 * s + 1)
+        c0, s0 = turn_cos_sin((middle + side_f) * off_x + freq_yf * off_y)
+        cd, sd = turn_cos_sin(TILE_KX * off_x)
+        ec_p[at_rows, :], es_p[at_rows, :] = c0, s0
+        ec_m[at_rows, :], es_m[at_rows, :] = c0 * cd + s0 * sd, s0 * cd - c0 * sd
+        dc[at_rows, :], ds[at_rows, :] = cd, sd
+    group_of = column(2 * shifts)[:, :3 * groups].astype(jnp.int32)
+    lane_group = lax.broadcasted_iota(jnp.int32, (rows, 3 * groups), 1) % groups
+    one_hot = (group_of == lane_group).astype(jnp.float32).astype(jnp.bfloat16)
+    limit = column(2 * shifts + 1)
+    limit_sq = limit * limit
+
+    cross[...] = jnp.zeros_like(cross)
+    norm[...] = jnp.zeros_like(norm)
+
+    def tile_step(tile, ec, es, sign):
+        re_cols = pl.ds(pl.multiple_of(tile * LANES, LANES), LANES)
+        im_cols = pl.ds(pl.multiple_of(half_width + tile * LANES, LANES), LANES)
+        two = pl.ds(pl.multiple_of(tile * 2 * LANES, 2 * LANES), 2 * LANES)
+        x_re, x_im = image[:, re_cols], image[:, im_cols]
+        c = jnp.dot(one_hot, tabs[:, re_cols], preferred_element_type=jnp.float32)
+        w = jnp.dot(one_hot, tabs[:, im_cols], preferred_element_type=jnp.float32)
+        freq_x = (TILE_KX * tile + side).astype(jnp.float32)
+        w = jnp.where(freq_x * freq_x + freq_yf * freq_yf < limit_sq, w, 0.0)
+        wc = w * c
+        norm[...] += w * (x_re * x_re + x_im * x_im)
+        quad_w[:, re_cols] = wc * c
+        u_re, u_im = wc * x_re, wc * x_im
+        for s in range(shifts):
+            at_rows = slice(s * rows, (s + 1) * rows)
+            ck, sk = ec[at_rows, :], es[at_rows, :]
+            wbuf[at_rows, pl.ds(pl.multiple_of(tile * 2 * LANES, LANES), LANES)] = (
+                u_re * ck + u_im * sk).astype(jnp.bfloat16)
+            wbuf[at_rows, pl.ds(pl.multiple_of(tile * 2 * LANES + LANES, LANES), LANES)] = (
+                u_im * ck - u_re * sk).astype(jnp.bfloat16)
+            cd, sd = dc[at_rows, :], ds[at_rows, :] * sign
+            ec[at_rows, :] = ck * cd - sk * sd
+            es[at_rows, :] = sk * cd + ck * sd
+        p_tile = jnp.concatenate(
+            [jnp.concatenate([proj_ref[k, :, re_cols], proj_ref[k, :, im_cols]], axis=1)
+             for k in range(proj_ref.shape[0])], axis=0)
+        cross[...] += lax.dot_general(
+            wbuf[:, two], p_tile, (((1,), (1,)), ((), ())), preferred_element_type=jnp.float32)
+
+    @pl.loop(0, tiles // 2)
+    def _(m):
+        tile_step(tiles // 2 + m, ec_p, es_p, 1.0)
+        tile_step(tiles // 2 - 1 - m, ec_m, es_m, -1.0)
+
+    quad = lax.dot_general(
+        quad_w[...], power[...], (((1,), (1,)), ((), ())),
+        precision=lax.Precision.HIGHEST, preferred_element_type=jnp.float32)
+    base = jnp.sum(norm[...], axis=1, keepdims=True) + quad
+    scale = 0.5 / math.sqrt(half_width)
+    scores = [-(base - 2.0 * cross[s * rows:(s + 1) * rows, :]) * scale for s in range(shifts)]
+    top = functools.reduce(jnp.maximum, scores)
+    top = jnp.max(top, axis=1, keepdims=True)
+    total = sum(jnp.exp(score - top) for score in scores)
+    total = jnp.sum(total, axis=1, keepdims=True)
+
+    mid = LANES // 2
+    row = jnp.where(lane == sub, top, 0.0) + jnp.where(lane == sub + mid, total, 0.0)
+    stats[me] = jnp.sum(row, axis=0, keepdims=True)
+    stat_copies = []
+    for step in range(1, n):
+        copy = pltpu.make_async_remote_copy(
+            src_ref=stats.at[me], dst_ref=stats.at[me],
+            send_sem=stat_send.at[step], recv_sem=stat_recv.at[me],
+            device_id={"blk": (me + step) % n},
+        )
+        copy.start()
+        stat_copies.append(copy)
+    for step in range(1, n):
+        slot = (me + n - step) % n
+        pltpu.make_async_remote_copy(
+            src_ref=stats.at[slot], dst_ref=stats.at[slot],
+            send_sem=stat_send.at[step], recv_sem=stat_recv.at[slot],
+            device_id={"blk": (me + step) % n},
+        ).wait_recv()
+    tops = jnp.concatenate([stats[d] for d in range(n)], axis=0)
+    totals = pltpu.roll(tops, mid, 1)
+    best = jnp.max(tops, axis=0, keepdims=True)
+    all_total = jnp.sum(totals * jnp.exp(tops - best), axis=0, keepdims=True)
+    log_row = best + jnp.log(all_total)
+    log_total = jnp.sum(jnp.where(lane == sub, log_row, 0.0), axis=1, keepdims=True)
+    best_row = jnp.exp(best - log_row)
+    lane_one = lax.broadcasted_iota(jnp.int32, (1, LANES), 1)
+    for p in range(own_rows):
+        mine = lane_one == me * own_rows + p
+        best_ref[p] = jnp.sum(jnp.where(mine, best_row, 0.0))
+        log_ref[p] = jnp.sum(jnp.where(mine, log_row, 0.0))
+
+    posterior = jnp.concatenate([jnp.exp(score - log_total) for score in scores], axis=0)
+    posterior = posterior.T.astype(jnp.bfloat16)
+    gain = proj_ref.shape[0] * proj_rows / own_rows
+
+    @pl.loop(0, tiles)
+    def _(tile):
+        two = pl.ds(pl.multiple_of(tile * 2 * LANES, 2 * LANES), 2 * LANES)
+        part = jnp.dot(posterior, wbuf[:, two], preferred_element_type=jnp.float32) * gain
+        for k in range(proj_ref.shape[0]):
+            block = part[k * proj_rows:(k + 1) * proj_rows]
+            out_ref[k, :, pl.ds(pl.multiple_of(tile * LANES, LANES), LANES)] = block[:, :LANES]
+            out_ref[k, :, pl.ds(pl.multiple_of(half_width + tile * LANES, LANES), LANES)] = block[:, LANES:]
+
+    for copy in sends + stat_copies:
+        copy.wait_send()
+
+
+def fused(n, projections, images, ctf_group, shift_offsets, shell_limit, ctf_table, noise_weight):
+    batches, orient, full = projections.shape
+    half_width = full // 2
+    own_rows, shifts = shift_offsets.shape[:2]
+    rows, cand = n * own_rows, batches * orient
+    na, nb = grid_sides(n)
+    groups = ctf_table.shape[0]
+    vmem, smem = pl.BlockSpec(memory_space=pltpu.VMEM), pl.BlockSpec(memory_space=pltpu.SMEM)
+    f32, bf16 = jnp.float32, jnp.bfloat16
+    table = pltpu.VMEM((shifts * rows, LANES), f32)
+    return pl.pallas_call(
+        functools.partial(kernel, (n, na, nb, rows, shifts, half_width)),
+        out_shape=(
+            jax.ShapeDtypeStruct(projections.shape, f32),
+            jax.ShapeDtypeStruct((own_rows,), f32),
+            jax.ShapeDtypeStruct((own_rows,), f32),
+        ),
+        in_specs=[vmem, vmem, smem, smem, smem, vmem, vmem],
+        out_specs=(vmem, smem, smem),
+        scratch_shapes=[
+            pltpu.VMEM((n, own_rows, full + LANES), bf16),
+            pltpu.VMEM((rows, full + LANES), f32),
+            pltpu.VMEM((cand, half_width), f32),
+            pltpu.VMEM((rows, half_width), f32),
+            pltpu.VMEM((3 * groups, full), bf16),
+            table, table, table, table, table, table,
+            pltpu.VMEM((shifts * rows, full), bf16),
+            pltpu.VMEM((shifts * rows, cand), f32),
+            pltpu.VMEM((rows, LANES), f32),
+            pltpu.VMEM((n, 1, LANES), f32),
+            pltpu.SemaphoreType.DMA((n,)),
+            pltpu.SemaphoreType.DMA((n,)),
+            pltpu.SemaphoreType.DMA((n,)),
+            pltpu.SemaphoreType.DMA((n,)),
+        ],
+        compiler_params=pltpu.CompilerParams(
+            collective_id=0, has_side_effects=True, vmem_limit_bytes=VMEM_LIMIT),
+    )(projections, images, ctf_group, shift_offsets, shell_limit, ctf_table, noise_weight)
+
+
+def per_device(n, *args):
+    particles = n * args[1].shape[0]
+    if particles > LANES // 2:
+        return local(*args)
+    return fused(n, *args)
+
+
 def solution(mesh):
     in_specs = (
         P(None, ("groups", "blk"), None),
@@ -182,4 +476,7 @@
         P("groups", None),
     )
     out_specs = (P(None, ("groups", "blk"), None), P(("groups", "blk")), P(("groups", "blk")))
-    return jax.shard_map(local, mesh=mesh, in_specs=in_specs, out_specs=out_specs, check_vma=False)
+    return jax.shard_map(
+        functools.partial(per_device, mesh.shape["blk"]),
+        mesh=mesh, in_specs=in_specs, out_specs=out_specs, check_vma=False,
+    )

time: 127 us -> 42.8 us (0.34)
  blocking collectives: 81.9 us -> 0 us
  Pallas kernels: 0 us -> 35.4 us
  other arithmetic: 15 us -> 0 us
  local copies, waits for them, and re-layouts: 18.9 us -> 6.48 us
  matrix products: 8.79 us -> 0 us
  between operations: 2.1 us -> 0.67 us
    all_gather x2 -> x0, blocking collectives: 42.4 us -> none  [the longest x1 23.6 us: local(): lax.all_gather(shift_offsets, 'blk', axis=0, tiled=True)]
    unnamed x2 -> x0, blocking collectives: 39.5 us -> none
    pallas_call x0 -> x1, Pallas kernels: none -> 35.4 us  [fused(): pl.pallas_call(functools.partial(kernel, (n, na, nb, rows, shifts, half_w...]
    dot_general x5 -> x0, matrix products: 8.79 us -> none  [the longest x1 3.63 us: add_block(): lax.dot_general(posterior, weighted, (((0, 1), (0, 1)), ((), ())), prefer...]
    sub x1 -> x0, local copies, waits for them, and re-layouts: 8.36 us -> none  [shift_factors(): cosine = cosine_x * cosine_y - sine_x * sine_y]
    add x1 -> x0, local copies, waits for them, and re-layouts: 8.32 us -> none  [shift_factors(): sine_part = sine_x * cosine_y + cosine_x * sine_y]
    sub x2 -> x0, other arithmetic: 7.17 us -> none  [the longest x1 7.17 us: shift_factors(): cosine = cosine_x * cosine_y - sine_x * sine_y]
    unnamed x26 -> x16, local copies, waits for them, and re-layouts: 1.78 us -> 6.48 us
where the time goes in v1:
time: 42.8 us; the launch traced here: 42.5 us
  Pallas kernels  35.4 us (83%)
  local copies, waits for them, and re-layouts  6.48 us (15%)
  between operations  0.67 us (2%)
    pallas_call x1, Pallas kernels, fused(): pl.pallas_call(functools.partial(kernel, (n, na, nb, rows, shifts, half_w...  35.4 us
    unnamed x16, local copies, waits for them, and re-layouts  6.48 us

profile of v1, /device:TPU:0, one launch (start us, length us, event | category | flops | bytes accessed | tf_op | source)
XLA Modules:
  0.0 42.5 jit_solution(6883643725057527347)
XLA Ops:
  0.6 0.0 copy-start.5
  0.6 0.0 copy-start.4
  0.7 0.8 %copy.10.off_ref = s32[2,9,2]{2,1,0:T(8,128)S(1)} copy(s32[2,9,2]{1,2,0:T(2,128)} %param.10) | data formatting | bytes 288 | tf_op args[3]
  1.4 0.0 copy-done.5
  1.4 0.0 copy-done.4
  1.4 0.0 copy-start
  1.5 1.0 %copy-done = bf16[2,16,8192]{2,1,0:T(8,128)(2,1)S(1)} copy-done((bf16[2,16,8192]{2,1,0:T(8,128)(2,1)S(1)}, bf16[2,16,8192]{2,1,0:T(8,128)(2,1)}, u32[]{:S(2)}) %copy-start) | copy-done | bytes 524312
  2.5 0.0 copy-start.1
  2.5 0.9 %copy-done.1 = f32[16,4096]{1,0:T(8,128)S(1)} copy-done((f32[16,4096]{1,0:T(8,128)S(1)}, f32[16,4096]{1,0:T(8,128)}, u32[]{:S(2)}) %copy-start.1) | copy-done | bytes 262168
  3.4 0.0 copy-start.2
  3.4 0.9 %copy-done.2 = f32[16,4096]{1,0:T(8,128)S(1)} copy-done((f32[16,4096]{1,0:T(8,128)S(1)}, f32[16,4096]{1,0:T(8,128)}, u32[]{:S(2)}) %copy-start.2) | copy-done | bytes 262168
  4.4 0.0 copy-start.3
  4.4 0.8 %copy-done.3 = bf16[2,8192]{1,0:T(2,128)(2,1)S(1)} copy-done((bf16[2,8192]{1,0:T(2,128)(2,1)S(1)}, bf16[2,8192]{1,0:T(2,128)(2,1)}, u32[]{:S(2)}) %copy-start.3) | copy-done | bytes 32792
  5.1 35.4 %shard_map.94 = (f32[2,16,8192]{2,1,0:T(8,128)S(1)}, f32[2]{0:T(128)S(1)}, f32[2]{0:T(128)S(1)}) custom-call(bf16[2,16,8192]{2,1,0:T(8,128)(2,1)S(1)} %copy-done, bf16[2,8192]{1,0:T(2,128)(2,1)S(1)} %copy-done.3, s32[2]{0:T(128)S(1)} %copy-done.4, s32[2,9,2]{2,1,0:T(8,128)S(1)} %copy.10.off_ref, s32[2]{0:T(128)S(1)} %copy-done.5, f32[16,4096]{1,0:T(8,128)S(1)} %copy-done.1, ...), custom_call_target="tpu_custom_call" | custom-call | tf_op jit(solution)/shard_map/pallas_call | solution.py:431
  40.5 1.0 %copy.14 = f32[2,16,8192]{2,1,0:T(8,128)} copy(f32[2,16,8192]{2,1,0:T(8,128)S(1)} %get-tuple-element.6) | data formatting | bytes 2097152
  41.5 0.5 %copy.15 = f32[2]{0:T(128)} copy(f32[2]{0:T(128)S(1)} %get-tuple-element.7) | data formatting | bytes 16
  42.0 0.5 %copy.16 = f32[2]{0:T(128)} copy(f32[2]{0:T(128)S(1)} %get-tuple-element.8) | data formatting | bytes 16
Async XLA Ops:
  0.6 0.8 %copy-start.5 = (s32[2]{0:T(128)S(1)}, s32[2]{0:T(128)}, u32[]{:S(2)}) copy-start(s32[2]{0:T(128)} %lim_ref.1) | copy-start | bytes 28
  0.6 0.8 %copy-start.4 = (s32[2]{0:T(128)S(1)}, s32[2]{0:T(128)}, u32[]{:S(2)}) copy-start(s32[2]{0:T(128)} %grp_ref.1) | copy-start | bytes 28
  1.4 1.0 %copy-start = (bf16[2,16,8192]{2,1,0:T(8,128)(2,1)S(1)}, bf16[2,16,8192]{2,1,0:T(8,128)(2,1)}, u32[]{:S(2)}) copy-start(bf16[2,16,8192]{2,1,0:T(8,128)(2,1)} %proj_ref.1) | copy-start | bytes 1572868
  2.5 0.9 %copy-start.1 = (f32[16,4096]{1,0:T(8,128)S(1)}, f32[16,4096]{1,0:T(8,128)}, u32[]{:S(2)}) copy-start(f32[16,4096]{1,0:T(8,128)} %ctf_ref.1) | copy-start | bytes 786436
  3.4 0.9 %copy-start.2 = (f32[16,4096]{1,0:T(8,128)S(1)}, f32[16,4096]{1,0:T(8,128)}, u32[]{:S(2)}) copy-start(f32[16,4096]{1,0:T(8,128)} %noise_ref.1) | copy-start | bytes 786436
  4.4 0.8 %copy-start.3 = (bf16[2,8192]{1,0:T(2,128)(2,1)S(1)}, bf16[2,8192]{1,0:T(2,128)(2,1)}, u32[]{:S(2)}) copy-start(bf16[2,8192]{1,0:T(2,128)(2,1)} %img_ref.1) | copy-start | bytes 98308

commit v2 on v1

--- a/solution.py
+++ b/solution.py
@@ -176,7 +176,7 @@
 
 LANES = 128
 TILE_KX = LANES // KY
-VMEM_LIMIT = 48 * 1024 * 1024
+VMEM_LIMIT = 60 * 1024 * 1024
 
 
 def turn_cos_sin(turns):
@@ -209,10 +209,11 @@
 
 def kernel(
     sizes,
-    proj_ref, img_ref, grp_ref, off_ref, lim_ref, ctf_ref, noise_ref,
-    out_ref, best_ref, log_ref,
-    pkt, image, power, quad_w, tabs, ec_p, es_p, ec_m, es_m, dc, ds, wbuf, cross, norm, stats,
-    send_sem, recv_sem, stat_send, stat_recv,
+    proj_hbm, img_hbm, grp_hbm, off_hbm, lim_hbm, ctf_hbm, noise_hbm,
+    out_hbm, best_ref, log_ref,
+    out_ref, proj_ref, grp_ref, off_ref, lim_ref, ctf_ref, noise_ref,
+    pkt, image, power, quad_w, tabs, ctf_rows, ec_p, es_p, ec_m, es_m, dc, ds, wbuf, stats,
+    load_sem, store_sem, send_sem, recv_sem, stat_send, stat_recv,
 ):
     n, na, nb, rows, shifts, half_width = sizes
     own_rows = rows // n
@@ -227,20 +228,33 @@
     def at(pa, pb, pc):
         return (pa * nb + pb) * 2 + pc
 
+    loads = [
+        pltpu.make_async_copy(source, target, load_sem.at[k])
+        for k, (source, target) in enumerate((
+            (grp_hbm, grp_ref), (off_hbm, off_ref), (lim_hbm, lim_ref),
+            (img_hbm, pkt.at[me, :, pl.ds(0, full)]),
+            (ctf_hbm, ctf_ref), (noise_hbm, noise_ref), (proj_hbm, proj_ref),
+        ))
+    ]
+    for load in loads:
+        load.start()
+
     barrier = pltpu.get_barrier_semaphore()
     for step in range(1, n):
         pl.semaphore_signal(barrier, inc=1, device_id={"blk": (me + step) % n})
 
     sub = lax.broadcasted_iota(jnp.int32, (own_rows, LANES), 0)
     lane = lax.broadcasted_iota(jnp.int32, (own_rows, LANES), 1)
+    for load in loads[:3]:
+        load.wait()
     meta = jnp.zeros((own_rows, LANES), jnp.float32)
     for p in range(own_rows):
-        entries = [off_ref[p, s, j] for s in range(shifts) for j in range(2)]
+        entries = [off_ref[p, j, s] for s in range(shifts) for j in range(2)]
         entries += [grp_ref[p], lim_ref[p]]
         for column, entry in enumerate(entries):
             meta = jnp.where((sub == p) & (lane == column), entry.astype(jnp.float32), meta)
-    pkt[me, :, :full] = img_ref[...]
     pkt[me, :, full:] = meta.astype(jnp.bfloat16)
+    loads[3].wait()
 
     pl.semaphore_wait(barrier, n - 1)
 
@@ -269,9 +283,18 @@
         send(me, at(a, (b + k) % nb, core))
     send(me, other)
 
+    plane = 2 * nb * own_rows
+
+    def widen(pa):
+        at_rows = pl.ds(pl.multiple_of(pa * plane, plane), plane)
+        image[at_rows, :] = jnp.concatenate(
+            [pkt[pa * nb * 2 + d].astype(jnp.float32) for d in range(2 * nb)], axis=0)
+
     for which, ref in enumerate((ctf_ref, noise_ref)):
+        loads[4 + which].wait()
         for part, value in enumerate(three_parts(ref[...])):
             tabs[part * groups:(part + 1) * groups, which * half_width:(which + 1) * half_width] = value
+    loads[6].wait()
     proj_rows = proj_ref.shape[1]
     for batch in range(proj_ref.shape[0]):
         real = proj_ref[batch, :, :half_width].astype(jnp.float32)
@@ -289,12 +312,11 @@
             slot = at((a + na - j) % na, (b + nb - k) % nb, core)
             arrived(slot)
             send(slot, other)
-    for k in range(nb):
-        for j in range(na):
-            arrived(at((a + na - j) % na, (b + nb - k) % nb, 1 - core))
-
-    for d in range(n):
-        image[d * own_rows:(d + 1) * own_rows, :] = pkt[d].astype(jnp.float32)
+    for j in range(na):
+        pa = (a + na - j) % na
+        for k in range(nb):
+            arrived(at(pa, (b + nb - k) % nb, 1 - core))
+        widen(pa)
 
     lane = lax.broadcasted_iota(jnp.int32, (rows, LANES), 1)
     sub = lax.broadcasted_iota(jnp.int32, (rows, LANES), 0)
@@ -321,47 +343,61 @@
     limit = column(2 * shifts + 1)
     limit_sq = limit * limit
 
-    cross[...] = jnp.zeros_like(cross)
-    norm[...] = jnp.zeros_like(norm)
-
-    def tile_step(tile, ec, es, sign):
-        re_cols = pl.ds(pl.multiple_of(tile * LANES, LANES), LANES)
-        im_cols = pl.ds(pl.multiple_of(half_width + tile * LANES, LANES), LANES)
-        two = pl.ds(pl.multiple_of(tile * 2 * LANES, 2 * LANES), 2 * LANES)
+    ctf_rows[...] = jnp.dot(one_hot, tabs[...], preferred_element_type=jnp.float32)
+    chunk = 4 * LANES
+    lane_chunk = lax.broadcasted_iota(jnp.int32, (rows, chunk), 1)
+    chunk_x = lane_chunk // KY
+    chunk_y = (lane_chunk % KY - KY // 2).astype(jnp.float32)
+    limit_chunk = jnp.concatenate([limit_sq] * (chunk // LANES), axis=1)
+
+    def weight_step(step, norm):
+        re_cols = pl.ds(pl.multiple_of(step * chunk, chunk), chunk)
+        im_cols = pl.ds(pl.multiple_of(half_width + step * chunk, chunk), chunk)
         x_re, x_im = image[:, re_cols], image[:, im_cols]
-        c = jnp.dot(one_hot, tabs[:, re_cols], preferred_element_type=jnp.float32)
-        w = jnp.dot(one_hot, tabs[:, im_cols], preferred_element_type=jnp.float32)
-        freq_x = (TILE_KX * tile + side).astype(jnp.float32)
-        w = jnp.where(freq_x * freq_x + freq_yf * freq_yf < limit_sq, w, 0.0)
+        c, w = ctf_rows[:, re_cols], ctf_rows[:, im_cols]
+        freq_x = (chunk // KY * step + chunk_x).astype(jnp.float32)
+        w = jnp.where(freq_x * freq_x + chunk_y * chunk_y < limit_chunk, w, 0.0)
         wc = w * c
-        norm[...] += w * (x_re * x_re + x_im * x_im)
         quad_w[:, re_cols] = wc * c
-        u_re, u_im = wc * x_re, wc * x_im
-        for s in range(shifts):
-            at_rows = slice(s * rows, (s + 1) * rows)
-            ck, sk = ec[at_rows, :], es[at_rows, :]
-            wbuf[at_rows, pl.ds(pl.multiple_of(tile * 2 * LANES, LANES), LANES)] = (
-                u_re * ck + u_im * sk).astype(jnp.bfloat16)
-            wbuf[at_rows, pl.ds(pl.multiple_of(tile * 2 * LANES + LANES, LANES), LANES)] = (
-                u_im * ck - u_re * sk).astype(jnp.bfloat16)
-            cd, sd = dc[at_rows, :], ds[at_rows, :] * sign
-            ec[at_rows, :] = ck * cd - sk * sd
-            es[at_rows, :] = sk * cd + ck * sd
-        p_tile = jnp.concatenate(
-            [jnp.concatenate([proj_ref[k, :, re_cols], proj_ref[k, :, im_cols]], axis=1)
-             for k in range(proj_ref.shape[0])], axis=0)
-        cross[...] += lax.dot_general(
-            wbuf[:, two], p_tile, (((1,), (1,)), ((), ())), preferred_element_type=jnp.float32)
-
-    @pl.loop(0, tiles // 2)
-    def _(m):
-        tile_step(tiles // 2 + m, ec_p, es_p, 1.0)
-        tile_step(tiles // 2 - 1 - m, ec_m, es_m, -1.0)
-
+        image[:, re_cols], image[:, im_cols] = wc * x_re, wc * x_im
+        return norm + w * (x_re * x_re + x_im * x_im)
+
+    norm = lax.fori_loop(0, half_width // chunk, weight_step, jnp.zeros((rows, chunk), jnp.float32))
+    norm = jnp.sum(norm, axis=1, keepdims=True)
+
+    depth = 4
+    for ec, es, sign in ((ec_p, es_p, 1), (ec_m, es_m, -1)):
+        first = tiles // 2 if sign > 0 else tiles // 2 - 1
+
+        @pl.loop(0, tiles // 2 // depth)
+        def _(m):
+            for r in range(0, rows, 16):
+                cols, factors = [], []
+                for q in range(depth):
+                    tile = first + sign * (m * depth + q)
+                    re_cols = pl.ds(pl.multiple_of(tile * LANES, LANES), LANES)
+                    im_cols = pl.ds(pl.multiple_of(half_width + tile * LANES, LANES), LANES)
+                    cols.append((re_cols, im_cols))
+                    factors.append((image[r:r + 16, re_cols], image[r:r + 16, im_cols]))
+                for s in range(shifts):
+                    at_rows = slice(s * rows + r, s * rows + r + 16)
+                    ck, sk, cd, sd = ec[at_rows, :], es[at_rows, :], dc[at_rows, :], ds[at_rows, :]
+                    for (re_cols, im_cols), (u_re, u_im) in zip(cols, factors):
+                        wbuf[at_rows, re_cols] = (u_re * ck + u_im * sk).astype(jnp.bfloat16)
+                        wbuf[at_rows, im_cols] = (u_im * ck - u_re * sk).astype(jnp.bfloat16)
+                        if sign > 0:
+                            ck, sk = ck * cd - sk * sd, sk * cd + ck * sd
+                        else:
+                            ck, sk = ck * cd + sk * sd, sk * cd - ck * sd
+                    ec[at_rows, :], es[at_rows, :] = ck, sk
+
+    p_rows = jnp.concatenate([proj_ref[k] for k in range(proj_ref.shape[0])], axis=0)
+    cross = lax.dot_general(
+        wbuf[...], p_rows, (((1,), (1,)), ((), ())), preferred_element_type=jnp.float32)
     quad = lax.dot_general(
         quad_w[...], power[...], (((1,), (1,)), ((), ())),
         precision=lax.Precision.HIGHEST, preferred_element_type=jnp.float32)
-    base = jnp.sum(norm[...], axis=1, keepdims=True) + quad
+    base = norm + quad
     scale = 0.5 / math.sqrt(half_width)
     scores = [-(base - 2.0 * cross[s * rows:(s + 1) * rows, :]) * scale for s in range(shifts)]
     top = functools.reduce(jnp.maximum, scores)
@@ -405,14 +441,24 @@
     posterior = posterior.T.astype(jnp.bfloat16)
     gain = proj_ref.shape[0] * proj_rows / own_rows
 
-    @pl.loop(0, tiles)
-    def _(tile):
-        two = pl.ds(pl.multiple_of(tile * 2 * LANES, 2 * LANES), 2 * LANES)
-        part = jnp.dot(posterior, wbuf[:, two], preferred_element_type=jnp.float32) * gain
+    wide = full // store_sem.shape[0]
+
+    def store(step):
+        cols = pl.ds(pl.multiple_of(step * wide, wide), wide)
+        return pltpu.make_async_copy(
+            out_ref.at[:, :, cols], out_hbm.at[:, :, cols], store_sem.at[step])
+
+    @pl.loop(0, full // wide)
+    def _(step):
+        cols = pl.ds(pl.multiple_of(step * wide, wide), wide)
+        part = jnp.dot(posterior, wbuf[:, cols], preferred_element_type=jnp.float32) * gain
         for k in range(proj_ref.shape[0]):
-            block = part[k * proj_rows:(k + 1) * proj_rows]
-            out_ref[k, :, pl.ds(pl.multiple_of(tile * LANES, LANES), LANES)] = block[:, :LANES]
-            out_ref[k, :, pl.ds(pl.multiple_of(half_width + tile * LANES, LANES), LANES)] = block[:, LANES:]
+            out_ref[k, :, cols] = part[k * proj_rows:(k + 1) * proj_rows]
+        store(step).start()
+
+    @pl.loop(0, full // wide)
+    def _(step):
+        store(step).wait()
 
     for copy in sends + stat_copies:
         copy.wait_send()
@@ -425,7 +471,7 @@
     rows, cand = n * own_rows, batches * orient
     na, nb = grid_sides(n)
     groups = ctf_table.shape[0]
-    vmem, smem = pl.BlockSpec(memory_space=pltpu.VMEM), pl.BlockSpec(memory_space=pltpu.SMEM)
+    smem = pl.BlockSpec(memory_space=pltpu.SMEM)
     f32, bf16 = jnp.float32, jnp.bfloat16
     table = pltpu.VMEM((shifts * rows, LANES), f32)
     return pl.pallas_call(
@@ -435,19 +481,27 @@
             jax.ShapeDtypeStruct((own_rows,), f32),
             jax.ShapeDtypeStruct((own_rows,), f32),
         ),
-        in_specs=[vmem, vmem, smem, smem, smem, vmem, vmem],
-        out_specs=(vmem, smem, smem),
+        in_specs=[pl.BlockSpec(memory_space=pltpu.HBM)] * 7,
+        out_specs=(pl.BlockSpec(memory_space=pltpu.HBM), smem, smem),
         scratch_shapes=[
+            pltpu.VMEM(projections.shape, f32),
+            pltpu.VMEM(projections.shape, bf16),
+            pltpu.SMEM(ctf_group.shape, jnp.int32),
+            pltpu.SMEM((own_rows, 2, shifts), jnp.int32),
+            pltpu.SMEM(shell_limit.shape, jnp.int32),
+            pltpu.VMEM(ctf_table.shape, f32),
+            pltpu.VMEM(noise_weight.shape, f32),
             pltpu.VMEM((n, own_rows, full + LANES), bf16),
             pltpu.VMEM((rows, full + LANES), f32),
             pltpu.VMEM((cand, half_width), f32),
             pltpu.VMEM((rows, half_width), f32),
             pltpu.VMEM((3 * groups, full), bf16),
+            pltpu.VMEM((rows, full), f32),
             table, table, table, table, table, table,
             pltpu.VMEM((shifts * rows, full), bf16),
-            pltpu.VMEM((shifts * rows, cand), f32),
-            pltpu.VMEM((rows, LANES), f32),
             pltpu.VMEM((n, 1, LANES), f32),
+            pltpu.SemaphoreType.DMA((7,)),
+            pltpu.SemaphoreType.DMA((8,)),
             pltpu.SemaphoreType.DMA((n,)),
             pltpu.SemaphoreType.DMA((n,)),
             pltpu.SemaphoreType.DMA((n,)),
@@ -455,7 +509,7 @@
         ],
         compiler_params=pltpu.CompilerParams(
             collective_id=0, has_side_effects=True, vmem_limit_bytes=VMEM_LIMIT),
-    )(projections, images, ctf_group, shift_offsets, shell_limit, ctf_table, noise_weight)
+    )(projections, images, ctf_group, shift_offsets.transpose(0, 2, 1), shell_limit, ctf_table, noise_weight)
 
 
 def per_device(n, *args):

time: 42.8 us -> 32.3 us (0.75)
  Pallas kernels: 35.4 us -> 28.1 us
  local copies, waits for them, and re-layouts: 6.48 us -> 3.35 us
    pallas_call x1, Pallas kernels: 35.4 us -> 28.1 us  [fused(): pl.pallas_call(functools.partial(kernel, (n, na, nb, rows, shifts, half_w...]
    unnamed x16 -> x7, local copies, waits for them, and re-layouts: 6.48 us -> 3.35 us
where the time goes in v2:
time: 32.3 us; the launch traced here: 32.1 us
  Pallas kernels  28.1 us (87%)
  local copies, waits for them, and re-layouts  3.35 us (10%)
  between operations  0.65 us (2%)
    pallas_call x1, Pallas kernels, fused(): pl.pallas_call(functools.partial(kernel, (n, na, nb, rows, shifts, half_w...  28.1 us
    unnamed x7, local copies, waits for them, and re-layouts  3.35 us

profile of v2, /device:TPU:0, one launch (start us, length us, event | category | flops | bytes accessed | tf_op | source)
XLA Modules:
  0.0 32.1 jit_solution(13316900162271221534)
XLA Ops:
  0.6 28.1 %shard_map.94 = (f32[2,16,8192]{2,1,0:T(8,128)}, f32[2]{0:T(128)}, f32[2]{0:T(128)}) custom-call(bf16[2,16,8192]{2,1,0:T(8,128)(2,1)} %proj_hbm.1, bf16[2,8192]{1,0:T(2,128)(2,1)} %img_hbm.1, s32[2]{0:T(128)} %grp_hbm.1, s32[2,2,9]{2,1,0:T(2,128)} %bitcast.1, s32[2]{0:T(128)} %lim_hbm.1, f32[16,4096]{1,0:T(8,128)} %ctf_hbm.1, f32[16,4096]{1,0:T(8,128)} %noise_hbm.1), custom_call_target="tpu_custom_call" | custom-call | tf_op jit(solution)/shard_map/pallas_call | solution.py:477
  28.8 0.0 copy-start.1
  28.8 2.3 %copy.13 = f32[2,16,8192]{2,1,0:T(8,128)} copy(f32[2,16,8192]{2,1,0:T(8,128)} %get-tuple-element.6) | data formatting | bytes 2097152
  31.0 0.0 copy-done.1
  31.0 0.0 copy-start
  31.0 0.5 %copy.14 = f32[2]{0:T(128)} copy(f32[2]{0:T(128)S(1)} %copy-done.1) | data formatting | bytes 16
  31.5 0.1 copy-done
  31.6 0.5 %copy.15 = f32[2]{0:T(128)} copy(f32[2]{0:T(128)S(1)} %copy-done) | data formatting | bytes 16
Async XLA Ops:
  28.8 2.3 %copy-start.1 = (f32[2]{0:T(128)S(1)}, f32[2]{0:T(128)}, u32[]{:S(2)}) copy-start(f32[2]{0:T(128)} %get-tuple-element.7) | copy-start | bytes 28
  31.0 0.6 %copy-start = (f32[2]{0:T(128)S(1)}, f32[2]{0:T(128)}, u32[]{:S(2)}) copy-start(f32[2]{0:T(128)} %get-tuple-element.8) | copy-start | bytes 28

commit v3 on v2

--- a/solution.py
+++ b/solution.py
@@ -207,32 +207,40 @@
     return outer, chips // outer
 
 
-def kernel(
+def score_kernel(
     sizes,
     proj_hbm, img_hbm, grp_hbm, off_hbm, lim_hbm, ctf_hbm, noise_hbm,
-    out_hbm, best_ref, log_ref,
-    out_ref, proj_ref, grp_ref, off_ref, lim_ref, ctf_ref, noise_ref,
-    pkt, image, power, quad_w, tabs, ctf_rows, ec_p, es_p, ec_m, es_m, dc, ds, wbuf, stats,
-    load_sem, store_sem, send_sem, recv_sem, stat_send, stat_recv,
+    post_ref, wide_hbm, best_ref, log_ref,
+    proj_ref, grp_ref, off_ref, lim_ref, ctf_ref, noise_ref,
+    pkt, notes, image, power, quad_w, quad, tabs, look, ec_p, es_p, ec_m, es_m, dc, ds, wbuf, score, stats,
+    load_sem, wide_sem, send_sem, recv_sem, note_send, note_recv, stat_send, stat_recv,
 ):
     n, na, nb, rows, shifts, half_width = sizes
     own_rows = rows // n
     full = 2 * half_width
     tiles = half_width // LANES
     groups = ctf_ref.shape[0]
+    plane = 2 * nb * own_rows
+    pairs, pair_rows = na // 2, 2 * plane
+    block = shifts * pair_rows
     me = lax.axis_index("blk")
     core = me % 2
     chip = me // 2
     a, b = chip // nb, chip % nb
+    other = me + 1 - 2 * core
 
     def at(pa, pb, pc):
         return (pa * nb + pb) * 2 + pc
+
+    def plane_at(step, half, sign):
+        pair = (a // 2 + pairs + sign * step) % pairs
+        return 2 * pair + (a % 2 if half == 0 else 1 - a % 2)
 
     loads = [
         pltpu.make_async_copy(source, target, load_sem.at[k])
         for k, (source, target) in enumerate((
             (grp_hbm, grp_ref), (off_hbm, off_ref), (lim_hbm, lim_ref),
-            (img_hbm, pkt.at[me, :, pl.ds(0, full)]),
+            (img_hbm, pkt.at[me]),
             (ctf_hbm, ctf_ref), (noise_hbm, noise_ref), (proj_hbm, proj_ref),
         ))
     ]
@@ -247,13 +255,13 @@
     lane = lax.broadcasted_iota(jnp.int32, (own_rows, LANES), 1)
     for load in loads[:3]:
         load.wait()
-    meta = jnp.zeros((own_rows, LANES), jnp.float32)
+    note = jnp.zeros((own_rows, LANES), jnp.float32)
     for p in range(own_rows):
         entries = [off_ref[p, j, s] for s in range(shifts) for j in range(2)]
         entries += [grp_ref[p], lim_ref[p]]
         for column, entry in enumerate(entries):
-            meta = jnp.where((sub == p) & (lane == column), entry.astype(jnp.float32), meta)
-    pkt[me, :, full:] = meta.astype(jnp.bfloat16)
+            note = jnp.where((sub == p) & (lane == column), entry.astype(jnp.float32), note)
+    notes[me] = note
     loads[3].wait()
 
     pl.semaphore_wait(barrier, n - 1)
@@ -276,19 +284,34 @@
             device_id={"blk": (me + 1) % n},
         ).wait_recv()
 
-    other = me + 1 - 2 * core
-    for j in range(1, na):
-        send(me, at((a + j) % na, b, core))
+    def swap(buffer, send_sems, recv_sems):
+        copies = []
+        for step in range(1, n):
+            copy = pltpu.make_async_remote_copy(
+                src_ref=buffer.at[me], dst_ref=buffer.at[me],
+                send_sem=send_sems.at[step], recv_sem=recv_sems.at[me],
+                device_id={"blk": (me + step) % n},
+            )
+            copy.start()
+            copies.append(copy)
+        return copies
+
+    def swapped(buffer, send_sems, recv_sems):
+        for step in range(1, n):
+            slot = (me + n - step) % n
+            pltpu.make_async_remote_copy(
+                src_ref=buffer.at[slot], dst_ref=buffer.at[slot],
+                send_sem=send_sems.at[step], recv_sem=recv_sems.at[slot],
+                device_id={"blk": (me + step) % n},
+            ).wait_recv()
+
+    far = [(step, half) for step in range(pairs) for half in range(2)][1:]
+    for step, half in far:
+        send(me, at(plane_at(step, half, 1), b, core))
     for k in range(1, nb):
         send(me, at(a, (b + k) % nb, core))
     send(me, other)
-
-    plane = 2 * nb * own_rows
-
-    def widen(pa):
-        at_rows = pl.ds(pl.multiple_of(pa * plane, plane), plane)
-        image[at_rows, :] = jnp.concatenate(
-            [pkt[pa * nb * 2 + d].astype(jnp.float32) for d in range(2 * nb)], axis=0)
+    note_copies = swap(notes, note_send, note_recv)
 
     for which, ref in enumerate((ctf_ref, noise_ref)):
         loads[4 + which].wait()
@@ -301,86 +324,118 @@
         imag = proj_ref[batch, :, half_width:].astype(jnp.float32)
         power[batch * proj_rows:(batch + 1) * proj_rows, :] = real * real + imag * imag
 
-    for j in range(1, na):
-        slot = at((a + na - j) % na, b, core)
+    def pass_plane(step, half):
+        slot = at(plane_at(step, half, -1), b, core)
         arrived(slot)
         for k in range(1, nb):
             send(slot, at(a, (b + k) % nb, core))
         send(slot, other)
-    for k in range(1, nb):
-        for j in range(na):
-            slot = at((a + na - j) % na, (b + nb - k) % nb, core)
+
+    def pass_side(step, half):
+        for k in range(1, nb):
+            slot = at(plane_at(step, half, -1), (b + nb - k) % nb, core)
             arrived(slot)
             send(slot, other)
-    for j in range(na):
-        pa = (a + na - j) % na
-        for k in range(nb):
-            arrived(at(pa, (b + nb - k) % nb, 1 - core))
-        widen(pa)
-
+
+    pass_plane(0, 1)
+    pass_side(0, 0)
+
+    swapped(notes, note_send, note_recv)
+    meta = jnp.concatenate([notes[d] for d in range(n)], axis=0)
     lane = lax.broadcasted_iota(jnp.int32, (rows, LANES), 1)
     sub = lax.broadcasted_iota(jnp.int32, (rows, LANES), 0)
-    side = lane // KY
-    freq_y = lane % KY - KY // 2
-    side_f, freq_yf = side.astype(jnp.float32), freq_y.astype(jnp.float32)
-    meta = image[:, full:]
+    side_f = (lane // KY).astype(jnp.float32)
+    freq_yf = (lane % KY - KY // 2).astype(jnp.float32)
 
     def column(j):
         return jnp.broadcast_to(meta[:, j:j + 1], (rows, LANES))
 
     middle = TILE_KX * (tiles // 2)
     for s in range(shifts):
-        at_rows = slice(s * rows, (s + 1) * rows)
         off_x, off_y = column(2 * s), column(2 * s + 1)
         c0, s0 = turn_cos_sin((middle + side_f) * off_x + freq_yf * off_y)
         cd, sd = turn_cos_sin(TILE_KX * off_x)
-        ec_p[at_rows, :], es_p[at_rows, :] = c0, s0
-        ec_m[at_rows, :], es_m[at_rows, :] = c0 * cd + s0 * sd, s0 * cd - c0 * sd
-        dc[at_rows, :], ds[at_rows, :] = cd, sd
+        cm, sm = c0 * cd + s0 * sd, s0 * cd - c0 * sd
+        for pair in range(pairs):
+            at_rows = slice(pair * block + s * pair_rows, pair * block + (s + 1) * pair_rows)
+            own = slice(pair * pair_rows, (pair + 1) * pair_rows)
+            for ref, value in ((ec_p, c0), (es_p, s0), (ec_m, cm), (es_m, sm), (dc, cd), (ds, sd)):
+                ref[at_rows, :] = value[own]
+
+    for step, half in far[1:]:
+        pass_plane(step, half)
+    pass_side(0, 1)
+
     group_of = column(2 * shifts)[:, :3 * groups].astype(jnp.int32)
     lane_group = lax.broadcasted_iota(jnp.int32, (rows, 3 * groups), 1) % groups
     one_hot = (group_of == lane_group).astype(jnp.float32).astype(jnp.bfloat16)
+    look[...] = jnp.dot(one_hot, tabs[...], preferred_element_type=jnp.float32)
     limit = column(2 * shifts + 1)
     limit_sq = limit * limit
-
-    ctf_rows[...] = jnp.dot(one_hot, tabs[...], preferred_element_type=jnp.float32)
     chunk = 4 * LANES
     lane_chunk = lax.broadcasted_iota(jnp.int32, (rows, chunk), 1)
     chunk_x = lane_chunk // KY
     chunk_y = (lane_chunk % KY - KY // 2).astype(jnp.float32)
     limit_chunk = jnp.concatenate([limit_sq] * (chunk // LANES), axis=1)
 
-    def weight_step(step, norm):
-        re_cols = pl.ds(pl.multiple_of(step * chunk, chunk), chunk)
-        im_cols = pl.ds(pl.multiple_of(half_width + step * chunk, chunk), chunk)
-        x_re, x_im = image[:, re_cols], image[:, im_cols]
-        c, w = ctf_rows[:, re_cols], ctf_rows[:, im_cols]
+    @pl.loop(0, half_width // chunk)
+    def _(step):
+        c_cols = pl.ds(pl.multiple_of(step * chunk, chunk), chunk)
+        w_cols = pl.ds(pl.multiple_of(half_width + step * chunk, chunk), chunk)
+        c, w = look[:, c_cols], look[:, w_cols]
         freq_x = (chunk // KY * step + chunk_x).astype(jnp.float32)
         w = jnp.where(freq_x * freq_x + chunk_y * chunk_y < limit_chunk, w, 0.0)
         wc = w * c
-        quad_w[:, re_cols] = wc * c
-        image[:, re_cols], image[:, im_cols] = wc * x_re, wc * x_im
-        return norm + w * (x_re * x_re + x_im * x_im)
-
-    norm = lax.fori_loop(0, half_width // chunk, weight_step, jnp.zeros((rows, chunk), jnp.float32))
-    norm = jnp.sum(norm, axis=1, keepdims=True)
-
+        quad_w[:, c_cols] = wc * c
+        look[:, c_cols], look[:, w_cols] = wc, w
+
+    for step, half in far[1:]:
+        pass_side(step, half)
+    quad[...] = lax.dot_general(
+        quad_w[...], power[...], (((1,), (1,)), ((), ())),
+        precision=lax.Precision.HIGHEST, preferred_element_type=jnp.float32)
+
+    scale = 0.5 / math.sqrt(half_width)
+    mid = LANES // 2
     depth = 4
-    for ec, es, sign in ((ec_p, es_p, 1), (ec_m, es_m, -1)):
-        first = tiles // 2 if sign > 0 else tiles // 2 - 1
-
-        @pl.loop(0, tiles // 2 // depth)
-        def _(m):
-            for r in range(0, rows, 16):
+    p_rows = jnp.concatenate([proj_ref[k] for k in range(proj_ref.shape[0])], axis=0)
+    stat_row = jnp.zeros((1, LANES), jnp.float32)
+    wide_copies = []
+    for pp in range(pairs):
+        pair = (a // 2 + pairs - pp) % pairs
+        for half in range(2):
+            pa = plane_at(pp, half, -1)
+            for k in range(nb):
+                arrived(at(pa, (b + nb - k) % nb, 1 - core))
+        norms = []
+        for half in range(2):
+            pa = 2 * pair + half
+            at_rows = pl.ds(pl.multiple_of(pa * plane, plane), plane)
+            x = jnp.concatenate(
+                [pkt[pa * nb * 2 + d].astype(jnp.float32) for d in range(2 * nb)], axis=0)
+            x_re, x_im = x[:, :half_width], x[:, half_width:]
+            wc, w = look[at_rows, :half_width], look[at_rows, half_width:]
+            image[at_rows, :half_width] = wc * x_re
+            image[at_rows, half_width:] = wc * x_im
+            norms.append(jnp.sum(w * (x_re * x_re + x_im * x_im), axis=1, keepdims=True))
+        norm = jnp.concatenate(norms, axis=0)
+        in_rows = pl.ds(pl.multiple_of(pair * pair_rows, pair_rows), pair_rows)
+        block_rows = pl.ds(pl.multiple_of(pair * block, block), block)
+
+        for ec, es, sign in ((ec_p, es_p, 1), (ec_m, es_m, -1)):
+            first = tiles // 2 if sign > 0 else tiles // 2 - 1
+
+            @pl.loop(0, tiles // 2 // depth)
+            def _(m):
                 cols, factors = [], []
                 for q in range(depth):
                     tile = first + sign * (m * depth + q)
                     re_cols = pl.ds(pl.multiple_of(tile * LANES, LANES), LANES)
                     im_cols = pl.ds(pl.multiple_of(half_width + tile * LANES, LANES), LANES)
                     cols.append((re_cols, im_cols))
-                    factors.append((image[r:r + 16, re_cols], image[r:r + 16, im_cols]))
+                    factors.append((image[in_rows, re_cols], image[in_rows, im_cols]))
                 for s in range(shifts):
-                    at_rows = slice(s * rows + r, s * rows + r + 16)
+                    at_rows = pl.ds(pl.multiple_of(pair * block + s * pair_rows, pair_rows), pair_rows)
                     ck, sk, cd, sd = ec[at_rows, :], es[at_rows, :], dc[at_rows, :], ds[at_rows, :]
                     for (re_cols, im_cols), (u_re, u_im) in zip(cols, factors):
                         wbuf[at_rows, re_cols] = (u_re * ck + u_im * sk).astype(jnp.bfloat16)
@@ -391,45 +446,36 @@
                             ck, sk = ck * cd + sk * sd, sk * cd - ck * sd
                     ec[at_rows, :], es[at_rows, :] = ck, sk
 
-    p_rows = jnp.concatenate([proj_ref[k] for k in range(proj_ref.shape[0])], axis=0)
-    cross = lax.dot_general(
-        wbuf[...], p_rows, (((1,), (1,)), ((), ())), preferred_element_type=jnp.float32)
-    quad = lax.dot_general(
-        quad_w[...], power[...], (((1,), (1,)), ((), ())),
-        precision=lax.Precision.HIGHEST, preferred_element_type=jnp.float32)
-    base = norm + quad
-    scale = 0.5 / math.sqrt(half_width)
-    scores = [-(base - 2.0 * cross[s * rows:(s + 1) * rows, :]) * scale for s in range(shifts)]
-    top = functools.reduce(jnp.maximum, scores)
-    top = jnp.max(top, axis=1, keepdims=True)
-    total = sum(jnp.exp(score - top) for score in scores)
-    total = jnp.sum(total, axis=1, keepdims=True)
-
-    mid = LANES // 2
-    row = jnp.where(lane == sub, top, 0.0) + jnp.where(lane == sub + mid, total, 0.0)
-    stats[me] = jnp.sum(row, axis=0, keepdims=True)
-    stat_copies = []
-    for step in range(1, n):
-        copy = pltpu.make_async_remote_copy(
-            src_ref=stats.at[me], dst_ref=stats.at[me],
-            send_sem=stat_send.at[step], recv_sem=stat_recv.at[me],
-            device_id={"blk": (me + step) % n},
-        )
+        copy = pltpu.make_async_copy(wbuf.at[block_rows], wide_hbm.at[block_rows], wide_sem.at[pp])
         copy.start()
-        stat_copies.append(copy)
-    for step in range(1, n):
-        slot = (me + n - step) % n
-        pltpu.make_async_remote_copy(
-            src_ref=stats.at[slot], dst_ref=stats.at[slot],
-            send_sem=stat_send.at[step], recv_sem=stat_recv.at[slot],
-            device_id={"blk": (me + step) % n},
-        ).wait_recv()
+        wide_copies.append(copy)
+        cross = lax.dot_general(
+            wbuf[block_rows, :], p_rows, (((1,), (1,)), ((), ())), preferred_element_type=jnp.float32)
+        base = norm + quad[in_rows, :]
+        scores = [-(base - 2.0 * cross[s * pair_rows:(s + 1) * pair_rows]) * scale for s in range(shifts)]
+        score[block_rows, :] = jnp.concatenate(scores, axis=0)
+        top = functools.reduce(jnp.maximum, scores)
+        top = jnp.max(top, axis=1, keepdims=True)
+        total = sum(jnp.exp(part - top) for part in scores)
+        total = jnp.sum(total, axis=1, keepdims=True)
+        spot = (lane - sub)[:pair_rows] - pair * pair_rows
+        row = jnp.where(spot == 0, top, 0.0) + jnp.where(spot == mid, total, 0.0)
+        stat_row = stat_row + jnp.sum(row, axis=0, keepdims=True)
+
+    stats[me] = stat_row
+    stat_copies = swap(stats, stat_send, stat_recv)
+    swapped(stats, stat_send, stat_recv)
     tops = jnp.concatenate([stats[d] for d in range(n)], axis=0)
     totals = pltpu.roll(tops, mid, 1)
     best = jnp.max(tops, axis=0, keepdims=True)
     all_total = jnp.sum(totals * jnp.exp(tops - best), axis=0, keepdims=True)
     log_row = best + jnp.log(all_total)
     log_total = jnp.sum(jnp.where(lane == sub, log_row, 0.0), axis=1, keepdims=True)
+    posterior = []
+    for pair in range(pairs):
+        own = jnp.concatenate([log_total[pair * pair_rows:(pair + 1) * pair_rows]] * shifts, axis=0)
+        posterior.append(jnp.exp(score[pair * block:(pair + 1) * block, :] - own))
+    post_ref[...] = jnp.concatenate(posterior, axis=0).T.astype(jnp.bfloat16)
     best_row = jnp.exp(best - log_row)
     lane_one = lax.broadcasted_iota(jnp.int32, (1, LANES), 1)
     for p in range(own_rows):
@@ -437,31 +483,18 @@
         best_ref[p] = jnp.sum(jnp.where(mine, best_row, 0.0))
         log_ref[p] = jnp.sum(jnp.where(mine, log_row, 0.0))
 
-    posterior = jnp.concatenate([jnp.exp(score - log_total) for score in scores], axis=0)
-    posterior = posterior.T.astype(jnp.bfloat16)
-    gain = proj_ref.shape[0] * proj_rows / own_rows
-
-    wide = full // store_sem.shape[0]
-
-    def store(step):
-        cols = pl.ds(pl.multiple_of(step * wide, wide), wide)
-        return pltpu.make_async_copy(
-            out_ref.at[:, :, cols], out_hbm.at[:, :, cols], store_sem.at[step])
-
-    @pl.loop(0, full // wide)
-    def _(step):
-        cols = pl.ds(pl.multiple_of(step * wide, wide), wide)
-        part = jnp.dot(posterior, wbuf[:, cols], preferred_element_type=jnp.float32) * gain
-        for k in range(proj_ref.shape[0]):
-            out_ref[k, :, cols] = part[k * proj_rows:(k + 1) * proj_rows]
-        store(step).start()
-
-    @pl.loop(0, full // wide)
-    def _(step):
-        store(step).wait()
-
-    for copy in sends + stat_copies:
+    for copy in sends + note_copies + stat_copies:
         copy.wait_send()
+    for copy in wide_copies:
+        copy.wait()
+
+
+def slice_kernel(gain, post_ref, wide_ref, best_ref, log_ref, out_ref, best_out, log_out):
+    part = jnp.dot(post_ref[...], wide_ref[...], preferred_element_type=jnp.float32) * gain
+    out_ref[...] = part.reshape(out_ref.shape)
+    for p in range(best_ref.shape[0]):
+        best_out[p] = best_ref[p]
+        log_out[p] = log_ref[p]
 
 
 def fused(n, projections, images, ctf_group, shift_offsets, shell_limit, ctf_table, noise_weight):
@@ -471,45 +504,59 @@
     rows, cand = n * own_rows, batches * orient
     na, nb = grid_sides(n)
     groups = ctf_table.shape[0]
-    smem = pl.BlockSpec(memory_space=pltpu.SMEM)
+    hbm, smem = pl.BlockSpec(memory_space=pltpu.HBM), pl.BlockSpec(memory_space=pltpu.SMEM)
+    vmem = pl.BlockSpec(memory_space=pltpu.VMEM)
     f32, bf16 = jnp.float32, jnp.bfloat16
     table = pltpu.VMEM((shifts * rows, LANES), f32)
-    return pl.pallas_call(
-        functools.partial(kernel, (n, na, nb, rows, shifts, half_width)),
+    pair_count = jax.ShapeDtypeStruct((own_rows,), f32)
+    posterior, wide, best, log_total = pl.pallas_call(
+        functools.partial(score_kernel, (n, na, nb, rows, shifts, half_width)),
         out_shape=(
-            jax.ShapeDtypeStruct(projections.shape, f32),
-            jax.ShapeDtypeStruct((own_rows,), f32),
-            jax.ShapeDtypeStruct((own_rows,), f32),
+            jax.ShapeDtypeStruct((cand, shifts * rows), bf16),
+            jax.ShapeDtypeStruct((shifts * rows, full), bf16),
+            pair_count,
+            pair_count,
         ),
-        in_specs=[pl.BlockSpec(memory_space=pltpu.HBM)] * 7,
-        out_specs=(pl.BlockSpec(memory_space=pltpu.HBM), smem, smem),
+        in_specs=[hbm] * 7,
+        out_specs=(vmem, hbm, smem, smem),
         scratch_shapes=[
-            pltpu.VMEM(projections.shape, f32),
             pltpu.VMEM(projections.shape, bf16),
             pltpu.SMEM(ctf_group.shape, jnp.int32),
             pltpu.SMEM((own_rows, 2, shifts), jnp.int32),
             pltpu.SMEM(shell_limit.shape, jnp.int32),
             pltpu.VMEM(ctf_table.shape, f32),
             pltpu.VMEM(noise_weight.shape, f32),
-            pltpu.VMEM((n, own_rows, full + LANES), bf16),
-            pltpu.VMEM((rows, full + LANES), f32),
+            pltpu.VMEM((n, own_rows, full), bf16),
+            pltpu.VMEM((n, own_rows, LANES), f32),
+            pltpu.VMEM((rows, full), f32),
             pltpu.VMEM((cand, half_width), f32),
             pltpu.VMEM((rows, half_width), f32),
+            pltpu.VMEM((rows, cand), f32),
             pltpu.VMEM((3 * groups, full), bf16),
             pltpu.VMEM((rows, full), f32),
             table, table, table, table, table, table,
             pltpu.VMEM((shifts * rows, full), bf16),
+            pltpu.VMEM((shifts * rows, cand), f32),
             pltpu.VMEM((n, 1, LANES), f32),
             pltpu.SemaphoreType.DMA((7,)),
-            pltpu.SemaphoreType.DMA((8,)),
-            pltpu.SemaphoreType.DMA((n,)),
-            pltpu.SemaphoreType.DMA((n,)),
-            pltpu.SemaphoreType.DMA((n,)),
-            pltpu.SemaphoreType.DMA((n,)),
-        ],
+            pltpu.SemaphoreType.DMA((na // 2,)),
+        ] + [pltpu.SemaphoreType.DMA((n,))] * 6,
         compiler_params=pltpu.CompilerParams(
             collective_id=0, has_side_effects=True, vmem_limit_bytes=VMEM_LIMIT),
     )(projections, images, ctf_group, shift_offsets.transpose(0, 2, 1), shell_limit, ctf_table, noise_weight)
+    columns = 1024
+    return pl.pallas_call(
+        functools.partial(slice_kernel, cand / own_rows),
+        grid=(full // columns,),
+        out_shape=(jax.ShapeDtypeStruct(projections.shape, f32), pair_count, pair_count),
+        in_specs=[
+            pl.BlockSpec((cand, shifts * rows), lambda k: (0, 0)),
+            pl.BlockSpec((shifts * rows, columns), lambda k: (0, k)),
+            smem, smem,
+        ],
+        out_specs=(pl.BlockSpec((batches, orient, columns), lambda k: (0, 0, k)), smem, smem),
+        compiler_params=pltpu.CompilerParams(vmem_limit_bytes=VMEM_LIMIT),
+    )(posterior, wide, best, log_total)
 
 
 def per_device(n, *args):

time: 32.3 us -> 35.8 us (1.11)
  Pallas kernels: 28.1 us -> 34.9 us
  local copies, waits for them, and re-layouts: 3.35 us -> 0 us
    pallas_call x1 -> x2, Pallas kernels: 28.1 us -> 34.9 us  [the longest x1 28.1 us: fused(): pl.pallas_call(functools.partial(score_kernel, (n, na, nb, rows, shifts,...]
    unnamed x7 -> x0, local copies, waits for them, and re-layouts: 3.35 us -> none
where the time goes in v3:
time: 35.8 us; the launch traced here: 35.5 us
  Pallas kernels  34.9 us (97%)
  between operations  0.64 us (2%)
    pallas_call x1, Pallas kernels, fused(): pl.pallas_call(functools.partial(score_kernel, (n, na, nb, rows, shifts,...  28.1 us
    pallas_call x1, Pallas kernels, fused(): pl.pallas_call(functools.partial(slice_kernel, cand / own_rows), grid=(fu...  6.8 us

profile of v3, /device:TPU:0, one launch (start us, length us, event | category | flops | bytes accessed | tf_op | source)
XLA Modules:
  0.0 35.5 jit_solution(13733665445387264262)
XLA Ops:
  0.6 28.1 %shard_map.94 = (bf16[32,288]{1,0:T(8,128)(2,1)}, bf16[288,8192]{1,0:T(8,128)(2,1)}, f32[2]{0:T(128)}, f32[2]{0:T(128)}) custom-call(bf16[2,16,8192]{2,1,0:T(8,128)(2,1)} %proj_hbm.1, bf16[2,8192]{1,0:T(2,128)(2,1)} %img_hbm.1, s32[2]{0:T(128)} %grp_hbm.1, s32[2,2,9]{2,1,0:T(2,128)} %bitcast.1, s32[2]{0:T(128)} %lim_hbm.1, f32[16,4096]{1,0:T(8,128)} %ctf_hbm.1, ...), custom_call_target="tpu_custom_call" | custom-call | tf_op jit(solution)/shard_map/pallas_call | solution.py:512
  28.7 6.8 %shard_map.95 = (f32[2,16,8192]{2,1,0:T(8,128)}, f32[2]{0:T(128)}, f32[2]{0:T(128)}) custom-call(bf16[32,288]{1,0:T(8,128)(2,1)} %get-tuple-element.7.post_ref, bf16[288,8192]{1,0:T(8,128)(2,1)} %get-tuple-element.8.wide_ref, f32[2]{0:T(128)} %get-tuple-element.9.best_ref, f32[2]{0:T(128)} %get-tuple-element.10.log_ref), custom_call_target="tpu_custom_call" | custom-call | tf_op jit(solution)/shard_map/pallas_call | solution.py:548

commit v4 on v2

--- a/solution.py
+++ b/solution.py
@@ -210,10 +210,10 @@
 def kernel(
     sizes,
     proj_hbm, img_hbm, grp_hbm, off_hbm, lim_hbm, ctf_hbm, noise_hbm,
-    out_hbm, best_ref, log_ref,
-    out_ref, proj_ref, grp_ref, off_ref, lim_ref, ctf_ref, noise_ref,
+    post_ref, wide_hbm, own_ref,
+    proj_ref, grp_ref, off_ref, lim_ref, ctf_ref, noise_ref,
     pkt, image, power, quad_w, tabs, ctf_rows, ec_p, es_p, ec_m, es_m, dc, ds, wbuf, stats,
-    load_sem, store_sem, send_sem, recv_sem, stat_send, stat_recv,
+    load_sem, wide_sem, send_sem, recv_sem, stat_send, stat_recv,
 ):
     n, na, nb, rows, shifts, half_width = sizes
     own_rows = rows // n
@@ -391,6 +391,8 @@
                             ck, sk = ck * cd + sk * sd, sk * cd - ck * sd
                     ec[at_rows, :], es[at_rows, :] = ck, sk
 
+    wide_copy = pltpu.make_async_copy(wbuf, wide_hbm, wide_sem)
+    wide_copy.start()
     p_rows = jnp.concatenate([proj_ref[k] for k in range(proj_ref.shape[0])], axis=0)
     cross = lax.dot_general(
         wbuf[...], p_rows, (((1,), (1,)), ((), ())), preferred_element_type=jnp.float32)
@@ -432,34 +434,16 @@
     log_total = jnp.sum(jnp.where(lane == sub, log_row, 0.0), axis=1, keepdims=True)
     best_row = jnp.exp(best - log_row)
     lane_one = lax.broadcasted_iota(jnp.int32, (1, LANES), 1)
-    for p in range(own_rows):
-        mine = lane_one == me * own_rows + p
-        best_ref[p] = jnp.sum(jnp.where(mine, best_row, 0.0))
-        log_ref[p] = jnp.sum(jnp.where(mine, log_row, 0.0))
+    for k, values in enumerate((best_row, log_row)):
+        picked = jnp.zeros((1, LANES), jnp.float32)
+        for p in range(own_rows):
+            mine = jnp.where(lane_one == me * own_rows + p, values, 0.0)
+            picked = jnp.where(lane_one == p, jnp.sum(mine, axis=1, keepdims=True), picked)
+        own_ref[k:k + 1, :] = picked
 
     posterior = jnp.concatenate([jnp.exp(score - log_total) for score in scores], axis=0)
-    posterior = posterior.T.astype(jnp.bfloat16)
-    gain = proj_ref.shape[0] * proj_rows / own_rows
-
-    wide = full // store_sem.shape[0]
-
-    def store(step):
-        cols = pl.ds(pl.multiple_of(step * wide, wide), wide)
-        return pltpu.make_async_copy(
-            out_ref.at[:, :, cols], out_hbm.at[:, :, cols], store_sem.at[step])
-
-    @pl.loop(0, full // wide)
-    def _(step):
-        cols = pl.ds(pl.multiple_of(step * wide, wide), wide)
-        part = jnp.dot(posterior, wbuf[:, cols], preferred_element_type=jnp.float32) * gain
-        for k in range(proj_ref.shape[0]):
-            out_ref[k, :, cols] = part[k * proj_rows:(k + 1) * proj_rows]
-        store(step).start()
-
-    @pl.loop(0, full // wide)
-    def _(step):
-        store(step).wait()
-
+    post_ref[...] = posterior.T.astype(jnp.bfloat16)
+    wide_copy.wait()
     for copy in sends + stat_copies:
         copy.wait_send()
 
@@ -471,20 +455,19 @@
     rows, cand = n * own_rows, batches * orient
     na, nb = grid_sides(n)
     groups = ctf_table.shape[0]
-    smem = pl.BlockSpec(memory_space=pltpu.SMEM)
+    vmem = pl.BlockSpec(memory_space=pltpu.VMEM)
     f32, bf16 = jnp.float32, jnp.bfloat16
     table = pltpu.VMEM((shifts * rows, LANES), f32)
-    return pl.pallas_call(
+    posterior, wide, own = pl.pallas_call(
         functools.partial(kernel, (n, na, nb, rows, shifts, half_width)),
         out_shape=(
-            jax.ShapeDtypeStruct(projections.shape, f32),
-            jax.ShapeDtypeStruct((own_rows,), f32),
-            jax.ShapeDtypeStruct((own_rows,), f32),
+            jax.ShapeDtypeStruct((cand, shifts * rows), bf16),
+            jax.ShapeDtypeStruct((shifts * rows, full), bf16),
+            jax.ShapeDtypeStruct((2, LANES), f32),
         ),
         in_specs=[pl.BlockSpec(memory_space=pltpu.HBM)] * 7,
-        out_specs=(pl.BlockSpec(memory_space=pltpu.HBM), smem, smem),
+        out_specs=(vmem, pl.BlockSpec(memory_space=pltpu.HBM), vmem),
         scratch_shapes=[
-            pltpu.VMEM(projections.shape, f32),
             pltpu.VMEM(projections.shape, bf16),
             pltpu.SMEM(ctf_group.shape, jnp.int32),
             pltpu.SMEM((own_rows, 2, shifts), jnp.int32),
@@ -501,7 +484,7 @@
             pltpu.VMEM((shifts * rows, full), bf16),
             pltpu.VMEM((n, 1, LANES), f32),
             pltpu.SemaphoreType.DMA((7,)),
-            pltpu.SemaphoreType.DMA((8,)),
+            pltpu.SemaphoreType.DMA,
             pltpu.SemaphoreType.DMA((n,)),
             pltpu.SemaphoreType.DMA((n,)),
             pltpu.SemaphoreType.DMA((n,)),
@@ -510,6 +493,8 @@
         compiler_params=pltpu.CompilerParams(
             collective_id=0, has_side_effects=True, vmem_limit_bytes=VMEM_LIMIT),
     )(projections, images, ctf_group, shift_offsets.transpose(0, 2, 1), shell_limit, ctf_table, noise_weight)
+    summed = jnp.dot(posterior, wide, preferred_element_type=f32) * (cand / own_rows)
+    return summed.reshape(projections.shape), own[0, :own_rows], own[1, :own_rows]
 
 
 def per_device(n, *args):

time: 32.3 us -> 31.3 us (0.969)
  matrix products: 0 us -> 4.32 us
  local copies, waits for them, and re-layouts: 3.35 us -> 0.52 us
  Pallas kernels: 28.1 us -> 25.6 us
    dot_general x0 -> x1, matrix products: none -> 4.32 us  [fused(): jnp.dot(posterior, wide, preferred_element_type=f32) * (cand / own_rows)]
    unnamed x7 -> x2, local copies, waits for them, and re-layouts: 3.35 us -> 0.01 us
    pallas_call x1, Pallas kernels: 28.1 us -> 25.6 us  [fused(): pl.pallas_call(functools.partial(kernel, (n, na, nb, rows, shifts, half_w...]
    squeeze x0 -> x1, local copies, waits for them, and re-layouts: none -> 0.52 us  [fused(): own[1, :own_rows]]
where the time goes in v4:
time: 31.3 us; the launch traced here: 31.1 us
  Pallas kernels  25.6 us (82%)
  matrix products  4.32 us (14%)
  between operations  0.65 us (2%)
  local copies, waits for them, and re-layouts  0.52 us (2%)
    pallas_call x1, Pallas kernels, fused(): pl.pallas_call(functools.partial(kernel, (n, na, nb, rows, shifts, half_w...  25.6 us
    dot_general x1, matrix products, fused(): jnp.dot(posterior, wide, preferred_element_type=f32) * (cand / own_rows)  4.32 us

profile of v4, /device:TPU:0, one launch (start us, length us, event | category | flops | bytes accessed | tf_op | source)
XLA Modules:
  0.0 31.1 jit_solution(6602247270754258231)
XLA Ops:
  0.6 25.6 %shard_map.94 = (bf16[32,288]{1,0:T(8,128)(2,1)}, bf16[288,8192]{1,0:T(8,128)(2,1)}, f32[2,128]{1,0:T(2,128)}) custom-call(bf16[2,16,8192]{2,1,0:T(8,128)(2,1)} %proj_hbm.1, bf16[2,8192]{1,0:T(2,128)(2,1)} %img_hbm.1, s32[2]{0:T(128)} %grp_hbm.1, s32[2,2,9]{2,1,0:T(2,128)} %bitcast.9, s32[2]{0:T(128)} %lim_hbm.1, f32[16,4096]{1,0:T(8,128)} %ctf_hbm.1, ...), custom_call_target="tpu_custom_call" | custom-call | tf_op jit(solution)/shard_map/pallas_call | solution.py:461
  26.3 0.0 copy-start
  26.3 4.3 %convolution_multiply_fusion = f32[32,8192]{1,0:T(8,128)} fusion(bf16[32,288]{1,0:T(8,128)(2,1)} %get-tuple-element.6, bf16[288,8192]{1,0:T(8,128)(2,1)} %get-tuple-element.7), kind=kOutput, calls=%fused_computation | convolution fusion | flops 151257088 | bytes 5785600 | tf_op jit(solution)/shard_map/dot_general | solution.py:496
  30.6 0.0 copy-done
  30.6 0.5 %slice_bitcast_fusion = (f32[2]{0:T(128)}, f32[2]{0:T(128)}) fusion(f32[2,128]{1,0:T(2,128)S(1)} %copy-done), kind=kLoop, calls=%fused_computation.1 | loop fusion | bytes 32 | tf_op jit(solution)/shard_map/squeeze | solution.py:497
Async XLA Ops:
  26.3 4.3 %copy-start = (f32[2,128]{1,0:T(2,128)S(1)}, f32[2,128]{1,0:T(2,128)}, u32[]{:S(2)}) copy-start(f32[2,128]{1,0:T(2,128)} %get-tuple-element.8) | copy-start | bytes 3076

commit v5 on v4

--- a/solution.py
+++ b/solution.py
@@ -176,7 +176,7 @@
 
 LANES = 128
 TILE_KX = LANES // KY
-VMEM_LIMIT = 60 * 1024 * 1024
+VMEM_LIMIT = 54 * 1024 * 1024
 
 
 def turn_cos_sin(turns):
@@ -210,10 +210,10 @@
 def kernel(
     sizes,
     proj_hbm, img_hbm, grp_hbm, off_hbm, lim_hbm, ctf_hbm, noise_hbm,
-    post_ref, wide_hbm, own_ref,
+    out_ref, own_ref,
     proj_ref, grp_ref, off_ref, lim_ref, ctf_ref, noise_ref,
     pkt, image, power, quad_w, tabs, ctf_rows, ec_p, es_p, ec_m, es_m, dc, ds, wbuf, stats,
-    load_sem, wide_sem, send_sem, recv_sem, stat_send, stat_recv,
+    load_sem, send_sem, recv_sem, stat_send, stat_recv,
 ):
     n, na, nb, rows, shifts, half_width = sizes
     own_rows = rows // n
@@ -299,7 +299,8 @@
     for batch in range(proj_ref.shape[0]):
         real = proj_ref[batch, :, :half_width].astype(jnp.float32)
         imag = proj_ref[batch, :, half_width:].astype(jnp.float32)
-        power[batch * proj_rows:(batch + 1) * proj_rows, :] = real * real + imag * imag
+        for part, value in enumerate(three_parts(real * real + imag * imag)):
+            power[part, batch * proj_rows:(batch + 1) * proj_rows, :] = value
 
     for j in range(1, na):
         slot = at((a + na - j) % na, b, core)
@@ -358,7 +359,8 @@
         freq_x = (chunk // KY * step + chunk_x).astype(jnp.float32)
         w = jnp.where(freq_x * freq_x + chunk_y * chunk_y < limit_chunk, w, 0.0)
         wc = w * c
-        quad_w[:, re_cols] = wc * c
+        for part, value in enumerate(three_parts(wc * c)):
+            quad_w[part * rows:(part + 1) * rows, re_cols] = value
         image[:, re_cols], image[:, im_cols] = wc * x_re, wc * x_im
         return norm + w * (x_re * x_re + x_im * x_im)
 
@@ -391,14 +393,15 @@
                             ck, sk = ck * cd + sk * sd, sk * cd - ck * sd
                     ec[at_rows, :], es[at_rows, :] = ck, sk
 
-    wide_copy = pltpu.make_async_copy(wbuf, wide_hbm, wide_sem)
-    wide_copy.start()
     p_rows = jnp.concatenate([proj_ref[k] for k in range(proj_ref.shape[0])], axis=0)
     cross = lax.dot_general(
         wbuf[...], p_rows, (((1,), (1,)), ((), ())), preferred_element_type=jnp.float32)
-    quad = lax.dot_general(
-        quad_w[...], power[...], (((1,), (1,)), ((), ())),
-        precision=lax.Precision.HIGHEST, preferred_element_type=jnp.float32)
+    quad = jnp.zeros((rows, power.shape[1]), jnp.float32)
+    for part in range(3):
+        product = lax.dot_general(
+            quad_w[:(3 - part) * rows, :], power[part], (((1,), (1,)), ((), ())),
+            preferred_element_type=jnp.float32)
+        quad = quad + sum(product[k * rows:(k + 1) * rows] for k in reversed(range(3 - part)))
     base = norm + quad
     scale = 0.5 / math.sqrt(half_width)
     scores = [-(base - 2.0 * cross[s * rows:(s + 1) * rows, :]) * scale for s in range(shifts)]
@@ -442,8 +445,18 @@
         own_ref[k:k + 1, :] = picked
 
     posterior = jnp.concatenate([jnp.exp(score - log_total) for score in scores], axis=0)
-    post_ref[...] = posterior.T.astype(jnp.bfloat16)
-    wide_copy.wait()
+    posterior = posterior.T.astype(jnp.bfloat16)
+    gain = proj_ref.shape[0] * proj_rows / own_rows
+
+    wide = 1024
+
+    @pl.loop(0, full // wide)
+    def _(step):
+        cols = pl.ds(pl.multiple_of(step * wide, wide), wide)
+        part = jnp.dot(posterior, wbuf[:, cols], preferred_element_type=jnp.float32) * gain
+        for k in range(proj_ref.shape[0]):
+            out_ref[k, :, cols] = part[k * proj_rows:(k + 1) * proj_rows]
+
     for copy in sends + stat_copies:
         copy.wait_send()
 
@@ -458,15 +471,14 @@
     vmem = pl.BlockSpec(memory_space=pltpu.VMEM)
     f32, bf16 = jnp.float32, jnp.bfloat16
     table = pltpu.VMEM((shifts * rows, LANES), f32)
-    posterior, wide, own = pl.pallas_call(
+    slices, own = pl.pallas_call(
         functools.partial(kernel, (n, na, nb, rows, shifts, half_width)),
         out_shape=(
-            jax.ShapeDtypeStruct((cand, shifts * rows), bf16),
-            jax.ShapeDtypeStruct((shifts * rows, full), bf16),
-            jax.ShapeDtypeStruct((2, LANES), f32),
+            pltpu.VMEM(projections.shape, f32),
+            pltpu.VMEM((2, LANES), f32),
         ),
         in_specs=[pl.BlockSpec(memory_space=pltpu.HBM)] * 7,
-        out_specs=(vmem, pl.BlockSpec(memory_space=pltpu.HBM), vmem),
+        out_specs=(vmem, vmem),
         scratch_shapes=[
             pltpu.VMEM(projections.shape, bf16),
             pltpu.SMEM(ctf_group.shape, jnp.int32),
@@ -476,15 +488,14 @@
             pltpu.VMEM(noise_weight.shape, f32),
             pltpu.VMEM((n, own_rows, full + LANES), bf16),
             pltpu.VMEM((rows, full + LANES), f32),
-            pltpu.VMEM((cand, half_width), f32),
-            pltpu.VMEM((rows, half_width), f32),
+            pltpu.VMEM((3, cand, half_width), bf16),
+            pltpu.VMEM((3 * rows, half_width), bf16),
             pltpu.VMEM((3 * groups, full), bf16),
             pltpu.VMEM((rows, full), f32),
             table, table, table, table, table, table,
             pltpu.VMEM((shifts * rows, full), bf16),
             pltpu.VMEM((n, 1, LANES), f32),
             pltpu.SemaphoreType.DMA((7,)),
-            pltpu.SemaphoreType.DMA,
             pltpu.SemaphoreType.DMA((n,)),
             pltpu.SemaphoreType.DMA((n,)),
             pltpu.SemaphoreType.DMA((n,)),
@@ -493,8 +504,7 @@
         compiler_params=pltpu.CompilerParams(
             collective_id=0, has_side_effects=True, vmem_limit_bytes=VMEM_LIMIT),
     )(projections, images, ctf_group, shift_offsets.transpose(0, 2, 1), shell_limit, ctf_table, noise_weight)
-    summed = jnp.dot(posterior, wide, preferred_element_type=f32) * (cand / own_rows)
-    return summed.reshape(projections.shape), own[0, :own_rows], own[1, :own_rows]
+    return slices, own[0, :own_rows], own[1, :own_rows]
 
 
 def per_device(n, *args):

time: 31.3 us -> 29.2 us (0.933)
  matrix products: 4.32 us -> 0 us
  Pallas kernels: 25.6 us -> 27 us
  local copies, waits for them, and re-layouts: 0.52 us -> 1.49 us
    dot_general x1 -> x0, matrix products: 4.32 us -> none  [fused(): jnp.dot(posterior, wide, preferred_element_type=f32) * (cand / own_rows)]
    pallas_call x1, Pallas kernels: 25.6 us -> 27 us  [fused(): pl.pallas_call(functools.partial(kernel, (n, na, nb, rows, shifts, half_w...]
    unnamed x2 -> x1, local copies, waits for them, and re-layouts: 0.01 us -> 0.97 us
where the time goes in v5:
time: 29.2 us; the launch traced here: 29.1 us
  Pallas kernels  27 us (92%)
  local copies, waits for them, and re-layouts  1.49 us (5%)
  between operations  0.64 us (2%)
    pallas_call x1, Pallas kernels, fused(): pl.pallas_call(functools.partial(kernel, (n, na, nb, rows, shifts, half_w...  27 us
    unnamed x1, local copies, waits for them, and re-layouts  0.97 us

profile of v5, /device:TPU:0, one launch (start us, length us, event | category | flops | bytes accessed | tf_op | source)
XLA Modules:
  0.0 29.1 jit_solution(4292309413931873709)
XLA Ops:
  0.6 27.0 %shard_map.94 = (f32[2,16,8192]{2,1,0:T(8,128)S(1)}, f32[2,128]{1,0:T(2,128)S(1)}) custom-call(bf16[2,16,8192]{2,1,0:T(8,128)(2,1)} %proj_hbm.1, bf16[2,8192]{1,0:T(2,128)(2,1)} %img_hbm.1, s32[2]{0:T(128)} %grp_hbm.1, s32[2,2,9]{2,1,0:T(2,128)} %bitcast.5, s32[2]{0:T(128)} %lim_hbm.1, f32[16,4096]{1,0:T(8,128)} %ctf_hbm.1, f32[16,4096]{1,0:T(8,128)} %noise_hbm.1), custom_call_target="tpu_custom_call" | custom-call | tf_op jit(solution)/shard_map/pallas_call | solution.py:474
  27.6 1.0 %copy.11 = f32[2,16,8192]{2,1,0:T(8,128)} copy(f32[2,16,8192]{2,1,0:T(8,128)S(1)} %get-tuple-element.9) | data formatting | bytes 2097152
  28.6 0.5 %slice_bitcast_fusion = (f32[2]{0:T(128)}, f32[2]{0:T(128)}) fusion(f32[2,128]{1,0:T(2,128)S(1)} %get-tuple-element.6), kind=kLoop, calls=%fused_computation | loop fusion | bytes 32 | tf_op jit(solution)/shard_map/squeeze | solution.py:507

commit v6 on v5

--- a/solution.py
+++ b/solution.py
@@ -176,6 +176,7 @@
 
 LANES = 128
 TILE_KX = LANES // KY
+BLOCK = 16
 VMEM_LIMIT = 54 * 1024 * 1024
 
 
@@ -212,7 +213,7 @@
     proj_hbm, img_hbm, grp_hbm, off_hbm, lim_hbm, ctf_hbm, noise_hbm,
     out_ref, own_ref,
     proj_ref, grp_ref, off_ref, lim_ref, ctf_ref, noise_ref,
-    pkt, image, power, quad_w, tabs, ctf_rows, ec_p, es_p, ec_m, es_m, dc, ds, wbuf, stats,
+    pkt, image, power, quad_w, tabs, ctf_rows, ec_p, es_p, ec_m, es_m, dc, ds, wbuf, stage, cross, stats,
     load_sem, send_sem, recv_sem, stat_send, stat_recv,
 ):
     n, na, nb, rows, shifts, half_width = sizes
@@ -368,34 +369,61 @@
     norm = jnp.sum(norm, axis=1, keepdims=True)
 
     depth = 4
+    span = depth * LANES
+    blocks = rows // BLOCK
+    cross[...] = jnp.zeros_like(cross)
+
+    def meet(block, base):
+        total = cross[block]
+        for k, start in enumerate((0, half_width)):
+            cols = pl.ds(pl.multiple_of(start + base * LANES, span), span)
+            p_cols = jnp.concatenate([proj_ref[batch, :, cols] for batch in range(proj_ref.shape[0])], axis=0)
+            total = total + lax.dot_general(
+                stage[block, :, k * span:(k + 1) * span], p_cols, (((1,), (1,)), ((), ())),
+                preferred_element_type=jnp.float32)
+        cross[block] = total
+
     for ec, es, sign in ((ec_p, es_p, 1), (ec_m, es_m, -1)):
-        first = tiles // 2 if sign > 0 else tiles // 2 - 1
-
-        @pl.loop(0, tiles // 2 // depth)
+        first = tiles // 2 if sign > 0 else tiles // 2 - depth
+        steps = tiles // 2 // depth
+        stage[blocks - 1] = jnp.zeros(stage.shape[1:], jnp.bfloat16)
+
+        @pl.loop(0, steps)
         def _(m):
-            for r in range(0, rows, 16):
+            base = first + sign * depth * m
+            base_before = first + sign * depth * jnp.maximum(m - 1, 0)
+            for block in range(blocks):
+                if block == 0:
+                    meet(blocks - 1, base_before)
+                else:
+                    meet(block - 1, base)
+                r = block * BLOCK
+                order = range(depth) if sign > 0 else range(depth - 1, -1, -1)
                 cols, factors = [], []
-                for q in range(depth):
-                    tile = first + sign * (m * depth + q)
+                for q in order:
+                    tile = base + q
                     re_cols = pl.ds(pl.multiple_of(tile * LANES, LANES), LANES)
                     im_cols = pl.ds(pl.multiple_of(half_width + tile * LANES, LANES), LANES)
-                    cols.append((re_cols, im_cols))
-                    factors.append((image[r:r + 16, re_cols], image[r:r + 16, im_cols]))
+                    cols.append((q, re_cols, im_cols))
+                    factors.append((image[r:r + BLOCK, re_cols], image[r:r + BLOCK, im_cols]))
                 for s in range(shifts):
-                    at_rows = slice(s * rows + r, s * rows + r + 16)
+                    at_rows = slice(s * rows + r, s * rows + r + BLOCK)
+                    in_stage = slice(s * BLOCK, (s + 1) * BLOCK)
                     ck, sk, cd, sd = ec[at_rows, :], es[at_rows, :], dc[at_rows, :], ds[at_rows, :]
-                    for (re_cols, im_cols), (u_re, u_im) in zip(cols, factors):
-                        wbuf[at_rows, re_cols] = (u_re * ck + u_im * sk).astype(jnp.bfloat16)
-                        wbuf[at_rows, im_cols] = (u_im * ck - u_re * sk).astype(jnp.bfloat16)
+                    for (q, re_cols, im_cols), (u_re, u_im) in zip(cols, factors):
+                        y_re = (u_re * ck + u_im * sk).astype(jnp.bfloat16)
+                        y_im = (u_im * ck - u_re * sk).astype(jnp.bfloat16)
+                        wbuf[at_rows, re_cols], wbuf[at_rows, im_cols] = y_re, y_im
+                        stage[block, in_stage, q * LANES:(q + 1) * LANES] = y_re
+                        stage[block, in_stage, span + q * LANES:span + (q + 1) * LANES] = y_im
                         if sign > 0:
                             ck, sk = ck * cd - sk * sd, sk * cd + ck * sd
                         else:
                             ck, sk = ck * cd + sk * sd, sk * cd - ck * sd
                     ec[at_rows, :], es[at_rows, :] = ck, sk
 
-    p_rows = jnp.concatenate([proj_ref[k] for k in range(proj_ref.shape[0])], axis=0)
-    cross = lax.dot_general(
-        wbuf[...], p_rows, (((1,), (1,)), ((), ())), preferred_element_type=jnp.float32)
+        meet(blocks - 1, first + sign * depth * (steps - 1))
+
     quad = jnp.zeros((rows, power.shape[1]), jnp.float32)
     for part in range(3):
         product = lax.dot_general(
@@ -404,7 +432,11 @@
         quad = quad + sum(product[k * rows:(k + 1) * rows] for k in reversed(range(3 - part)))
     base = norm + quad
     scale = 0.5 / math.sqrt(half_width)
-    scores = [-(base - 2.0 * cross[s * rows:(s + 1) * rows, :]) * scale for s in range(shifts)]
+    crosses = [
+        jnp.concatenate([cross[block, s * BLOCK:(s + 1) * BLOCK, :] for block in range(blocks)], axis=0)
+        for s in range(shifts)
+    ]
+    scores = [-(base - 2.0 * part) * scale for part in crosses]
     top = functools.reduce(jnp.maximum, scores)
     top = jnp.max(top, axis=1, keepdims=True)
     total = sum(jnp.exp(score - top) for score in scores)
@@ -494,6 +526,8 @@
             pltpu.VMEM((rows, full), f32),
             table, table, table, table, table, table,
             pltpu.VMEM((shifts * rows, full), bf16),
+            pltpu.VMEM((rows // BLOCK, shifts * BLOCK, 8 * LANES), bf16),
+            pltpu.VMEM((rows // BLOCK, shifts * BLOCK, cand), f32),
             pltpu.VMEM((n, 1, LANES), f32),
             pltpu.SemaphoreType.DMA((7,)),
             pltpu.SemaphoreType.DMA((n,)),
@@ -509,7 +543,7 @@
 
 def per_device(n, *args):
     particles = n * args[1].shape[0]
-    if particles > LANES // 2:
+    if particles > LANES // 2 or particles % BLOCK:
         return local(*args)
     return fused(n, *args)
 

time: 29.2 us -> 30.3 us (1.038)
  Pallas kernels: 27 us -> 28 us
    pallas_call x1, Pallas kernels: 27 us -> 28 us  [fused(): pl.pallas_call(functools.partial(kernel, (n, na, nb, rows, shifts, half_w...]
where the time goes in v6:
time: 30.3 us; the launch traced here: 30.1 us
  Pallas kernels  28 us (92%)
  local copies, waits for them, and re-layouts  1.49 us (5%)
  between operations  0.64 us (2%)
    pallas_call x1, Pallas kernels, fused(): pl.pallas_call(functools.partial(kernel, (n, na, nb, rows, shifts, half_w...  28 us
    unnamed x1, local copies, waits for them, and re-layouts  0.97 us

profile of v6, /device:TPU:0, one launch (start us, length us, event | category | flops | bytes accessed | tf_op | source)
XLA Modules:
  0.0 30.1 jit_solution(8470644263736710038)
XLA Ops:
  0.6 28.0 %shard_map.94 = (f32[2,16,8192]{2,1,0:T(8,128)S(1)}, f32[2,128]{1,0:T(2,128)S(1)}) custom-call(bf16[2,16,8192]{2,1,0:T(8,128)(2,1)} %proj_hbm.1, bf16[2,8192]{1,0:T(2,128)(2,1)} %img_hbm.1, s32[2]{0:T(128)} %grp_hbm.1, s32[2,2,9]{2,1,0:T(2,128)} %bitcast.5, s32[2]{0:T(128)} %lim_hbm.1, f32[16,4096]{1,0:T(8,128)} %ctf_hbm.1, f32[16,4096]{1,0:T(8,128)} %noise_hbm.1), custom_call_target="tpu_custom_call" | custom-call | tf_op jit(solution)/shard_map/pallas_call | solution.py:506
  28.6 1.0 %copy.11 = f32[2,16,8192]{2,1,0:T(8,128)} copy(f32[2,16,8192]{2,1,0:T(8,128)S(1)} %get-tuple-element.9) | data formatting | bytes 2097152
  29.6 0.5 %slice_bitcast_fusion = (f32[2]{0:T(128)}, f32[2]{0:T(128)}) fusion(f32[2,128]{1,0:T(2,128)S(1)} %get-tuple-element.6), kind=kLoop, calls=%fused_computation | loop fusion | bytes 32 | tf_op jit(solution)/shard_map/squeeze | solution.py:541

commit v7 on v5

--- a/solution.py
+++ b/solution.py
@@ -329,12 +329,14 @@
     def column(j):
         return jnp.broadcast_to(meta[:, j:j + 1], (rows, LANES))
 
+    turn_c, turn_s = turn_cos_sin(TILE_KX * meta)
     middle = TILE_KX * (tiles // 2)
     for s in range(shifts):
         at_rows = slice(s * rows, (s + 1) * rows)
         off_x, off_y = column(2 * s), column(2 * s + 1)
         c0, s0 = turn_cos_sin((middle + side_f) * off_x + freq_yf * off_y)
-        cd, sd = turn_cos_sin(TILE_KX * off_x)
+        cd = jnp.broadcast_to(turn_c[:, 2 * s:2 * s + 1], (rows, LANES))
+        sd = jnp.broadcast_to(turn_s[:, 2 * s:2 * s + 1], (rows, LANES))
         ec_p[at_rows, :], es_p[at_rows, :] = c0, s0
         ec_m[at_rows, :], es_m[at_rows, :] = c0 * cd + s0 * sd, s0 * cd - c0 * sd
         dc[at_rows, :], ds[at_rows, :] = cd, sd
@@ -450,9 +452,8 @@
 
     wide = 1024
 
-    @pl.loop(0, full // wide)
-    def _(step):
-        cols = pl.ds(pl.multiple_of(step * wide, wide), wide)
+    for step in range(full // wide):
+        cols = slice(step * wide, (step + 1) * wide)
         part = jnp.dot(posterior, wbuf[:, cols], preferred_element_type=jnp.float32) * gain
         for k in range(proj_ref.shape[0]):
             out_ref[k, :, cols] = part[k * proj_rows:(k + 1) * proj_rows]

time: 29.2 us -> 29.4 us (level)
  no operation moved by 1% of the time
where the time goes in v7:
time: 29.4 us; the launch traced here: 29.3 us
  Pallas kernels  27.1 us (92%)
  local copies, waits for them, and re-layouts  1.49 us (5%)
  between operations  0.64 us (2%)
    pallas_call x1, Pallas kernels, fused(): pl.pallas_call(functools.partial(kernel, (n, na, nb, rows, shifts, half_w...  27.1 us
    unnamed x1, local copies, waits for them, and re-layouts  0.97 us

profile of v7, /device:TPU:0, one launch (start us, length us, event | category | flops | bytes accessed | tf_op | source)
XLA Modules:
  0.0 29.3 jit_solution(11979430174117590679)
XLA Ops:
  0.6 27.1 %shard_map.94 = (f32[2,16,8192]{2,1,0:T(8,128)S(1)}, f32[2,128]{1,0:T(2,128)S(1)}) custom-call(bf16[2,16,8192]{2,1,0:T(8,128)(2,1)} %proj_hbm.1, bf16[2,8192]{1,0:T(2,128)(2,1)} %img_hbm.1, s32[2]{0:T(128)} %grp_hbm.1, s32[2,2,9]{2,1,0:T(2,128)} %bitcast.5, s32[2]{0:T(128)} %lim_hbm.1, f32[16,4096]{1,0:T(8,128)} %ctf_hbm.1, f32[16,4096]{1,0:T(8,128)} %noise_hbm.1), custom_call_target="tpu_custom_call" | custom-call | tf_op jit(solution)/shard_map/pallas_call | solution.py:475
  27.8 1.0 %copy.11 = f32[2,16,8192]{2,1,0:T(8,128)} copy(f32[2,16,8192]{2,1,0:T(8,128)S(1)} %get-tuple-element.9) | data formatting | bytes 2097152
  28.7 0.5 %slice_bitcast_fusion = (f32[2]{0:T(128)}, f32[2]{0:T(128)}) fusion(f32[2,128]{1,0:T(2,128)S(1)} %get-tuple-element.6), kind=kLoop, calls=%fused_computation | loop fusion | bytes 32 | tf_op jit(solution)/shard_map/squeeze | solution.py:508

commit v8 on v5

--- a/solution.py
+++ b/solution.py
@@ -367,7 +367,7 @@
     norm = lax.fori_loop(0, half_width // chunk, weight_step, jnp.zeros((rows, chunk), jnp.float32))
     norm = jnp.sum(norm, axis=1, keepdims=True)
 
-    depth = 4
+    depth = 8
     for ec, es, sign in ((ec_p, es_p, 1), (ec_m, es_m, -1)):
         first = tiles // 2 if sign > 0 else tiles // 2 - 1
 

time: 29.2 us -> 29.2 us (level)
  no operation moved by 1% of the time
where the time goes in v8:
time: 29.2 us; the launch traced here: 29.1 us
  Pallas kernels  27 us (92%)
  local copies, waits for them, and re-layouts  1.49 us (5%)
  between operations  0.64 us (2%)
    pallas_call x1, Pallas kernels, fused(): pl.pallas_call(functools.partial(kernel, (n, na, nb, rows, shifts, half_w...  27 us
    unnamed x1, local copies, waits for them, and re-layouts  0.97 us

profile of v8, /device:TPU:0, one launch (start us, length us, event | category | flops | bytes accessed | tf_op | source)
XLA Modules:
  0.0 29.1 jit_solution(8680165797737697566)
XLA Ops:
  0.6 27.0 %shard_map.94 = (f32[2,16,8192]{2,1,0:T(8,128)S(1)}, f32[2,128]{1,0:T(2,128)S(1)}) custom-call(bf16[2,16,8192]{2,1,0:T(8,128)(2,1)} %proj_hbm.1, bf16[2,8192]{1,0:T(2,128)(2,1)} %img_hbm.1, s32[2]{0:T(128)} %grp_hbm.1, s32[2,2,9]{2,1,0:T(2,128)} %bitcast.5, s32[2]{0:T(128)} %lim_hbm.1, f32[16,4096]{1,0:T(8,128)} %ctf_hbm.1, f32[16,4096]{1,0:T(8,128)} %noise_hbm.1), custom_call_target="tpu_custom_call" | custom-call | tf_op jit(solution)/shard_map/pallas_call | solution.py:474
  27.6 1.0 %copy.11 = f32[2,16,8192]{2,1,0:T(8,128)} copy(f32[2,16,8192]{2,1,0:T(8,128)S(1)} %get-tuple-element.9) | data formatting | bytes 2097152
  28.6 0.5 %slice_bitcast_fusion = (f32[2]{0:T(128)}, f32[2]{0:T(128)}) fusion(f32[2,128]{1,0:T(2,128)S(1)} %get-tuple-element.6), kind=kLoop, calls=%fused_computation | loop fusion | bytes 32 | tf_op jit(solution)/shard_map/squeeze | solution.py:507
